TPU v7x, 32 devices: a whole 2x2x4 slice. The times are simulated.
32 devices in a mesh: expert: 8 (over z, y), dp: 4 (over x, core).
Axes of the slice: x: 2, y: 2, z: 4, core: 2. Of those that a mesh axis runs over, the one named last changes fastest.
Arguments:
- grads: bfloat16 [4, 16, 128, 1536], P('dp', 'expert'), may hold values from -6 to 6
- master: float32 [8, 128, 1536], P('expert', 'dp'), may hold values from -0.12 to 0.12
- moment: float32 [8, 128, 1536], P('expert', 'dp'), may hold values from -0.4 to 0.4
- second: float32 [8, 128, 1536], P('expert', 'dp'), may hold values from 0.001 to 0.01
- old_place: int32 [8, 2], replicated, may hold values from 0 to 7, all different within a row
- new_place: int32 [8, 2], replicated, may hold values from 0 to 7, all different within a row
- owner_slot: int32 [8], replicated, may hold values from 0 to 7, as said below
Outputs:
- new_master: float32 [8, 128, 1536], P('expert', 'dp')
- new_moment: float32 [8, 128, 1536], P('expert', 'dp')
- new_second: float32 [8, 128, 1536], P('expert', 'dp')
- replicas: bfloat16 [16, 128, 1536], P('expert', 'dp')
Inputs may be any that keep to these rules, and one draw needn't show every extreme that they name: `owner_slot`: distinct values; the expert's owner is device value // 1 of the expert axis, in its owner slot value % 1. Slots that no expert names hold unused state. `old_place`: each device's 2 slots name distinct experts; every expert is named by some slot. `new_place`: each device's 2 slots name distinct experts; every expert is named by some slot.
All inputs are finite; a program needn't handle non-finite values.
Results may differ from a plain program's by a relative error of at most 0.015.
Values may be sent and summed in bfloat16 or wider, within the bound.
A program may use at most 64 MiB of HBM per device.

v0:
```python
import jax
import jax.numpy as jnp
from jax import lax
from jax.sharding import PartitionSpec as P

beta_first = 0.9
beta_second = 0.999
learn_rate = 0.02
weight_decay = 0.1
epsilon = 1e-08
scale_first = 1.0 - 0.9**40
scale_second = 1.0 - 0.999**40


def on_device(grads, master, moment, second, old_place, new_place, owner_slot):
    device_count = lax.axis_size("expert")
    slot_count = grads.shape[1]
    col_count = grads.shape[3]
    own_count = master.shape[0]
    quarter_rows = master.shape[1]
    piece_size = quarter_rows * col_count // device_count
    expert_count = owner_slot.shape[0]
    expert_ids = jnp.arange(expert_count, dtype=jnp.int32)
    old_hot = (expert_ids[:, None] == old_place.T.reshape(-1)[None, :]).astype(jnp.float32)
    summed = lax.psum_scatter(
        grads[0].astype(jnp.float32).astype(jnp.bfloat16), "dp", scatter_dimension=1, tiled=True
    ).astype(jnp.float32)
    incoming = lax.all_to_all(
        summed.reshape(slot_count, device_count, piece_size),
        "expert",
        split_axis=1,
        concat_axis=1,
        tiled=True,
    )
    expert_part = jnp.dot(
        old_hot,
        incoming.reshape(slot_count * device_count, piece_size),
        precision=lax.Precision.HIGHEST,
    )
    slot_ids = jnp.arange(device_count * own_count, dtype=jnp.int32)
    owner_hot = (
        (slot_ids[:, None] == owner_slot[None, :])
        .astype(jnp.float32)
        .reshape(device_count, own_count, expert_count)
    )
    outgoing = jnp.einsum("koe,ep->okp", owner_hot, expert_part, precision=lax.Precision.HIGHEST)
    slot_grad = lax.all_to_all(outgoing, "expert", split_axis=1, concat_axis=1, tiled=True).reshape(
        own_count, quarter_rows, col_count
    )
    new_moment = beta_first * moment + (1.0 - beta_first) * slot_grad
    new_second = beta_second * second + (1.0 - beta_second) * slot_grad * slot_grad
    update = new_moment / scale_first / (jnp.sqrt(new_second / scale_second) + epsilon)
    new_master = master - learn_rate * (update + weight_decay * master)
    fresh = new_master.astype(jnp.bfloat16).reshape(own_count, device_count, piece_size)
    every_slot = lax.all_to_all(fresh, "expert", split_axis=1, concat_axis=0, tiled=True).reshape(
        device_count * own_count, piece_size
    )
    wanted = owner_slot[new_place.T.reshape(-1)]
    outbound = jnp.take(every_slot, wanted, axis=0).reshape(slot_count, device_count, piece_size)
    received = lax.all_to_all(outbound, "expert", split_axis=1, concat_axis=1, tiled=True)
    replicas = received.reshape(slot_count, quarter_rows, col_count)
    return (new_master, new_moment, new_second, replicas)


def solution(mesh):
    placed = (
        P("dp", "expert", None, None),
        P("expert", "dp", None),
        P("expert", "dp", None),
        P("expert", "dp", None),
        P(),
        P(),
        P(),
    )
    return jax.shard_map(
        on_device,
        mesh=mesh,
        in_specs=placed,
        out_specs=(
            P("expert", "dp", None),
            P("expert", "dp", None),
            P("expert", "dp", None),
            P("expert", "dp", None),
        ),
        check_vma=False,
    )
```

profile of v0, /device:TPU:0, one launch (start us, length us, event | category | flops | bytes accessed | tf_op | source)
XLA Modules:
  0.0 103.2 jit_solution(7657351991952434953)
XLA Ops:
  7.2 0.7 reduce-scatter.2.cloned.1.call-update
  7.9 28.6 %reduce-scatter.2.cloned.1.call-done = bf16[2,32,1536]{2,1,0:T(8,128)(2,1)} async-done(((bf16[2,128,1536]{2,1,0:T(8,128)(2,1)}), bf16[2,32,1536]{2,1,0:T(8,128)(2,1)}) %reduce-scatter.2.cloned.1.call-update) | async-done | bytes 196624 | tf_op jit(solution)/shard_map/reduce_scatter | solution.py:25
  36.5 1.1 %reshape.149 = f32[2,8,6144]{2,1,0:T(8,128)S(1)} reshape(bf16[2,32,1536]{2,1,0:T(8,128)(2,1)} %reduce-scatter.2.cloned.1.call-done) | data formatting | bytes 589824 | tf_op jit(solution)/shard_map/reshape | solution.py:29
  37.6 1.0 %copy.14 = f32[2,8,6144]{2,0,1:T(2,128)} copy(f32[2,8,6144]{2,1,0:T(8,128)S(1)} %reshape.149) | data formatting | bytes 786432 | tf_op jit(solution)/shard_map/reshape | solution.py:29
  38.6 5.5 %all-to-all-start = ((f32[2,8,6144]{2,0,1:T(2,128)}), f32[2,8,6144]{2,0,1:T(2,128)S(1)}, u32[]{:S(2)}, u32[]{:S(2)}) async-start(f32[2,8,6144]{2,0,1:T(2,128)} %copy.14), calls=%async_computation.1 | async-start | bytes 786432 | tf_op jit(solution)/shard_map/all_to_all | solution.py:28
  44.1 0.7 copy-done.4
  44.8 0.1 eq.31
  44.9 0.7 copy-done.5
  45.6 0.1 reshape.144
  45.7 10.2 %all-to-all-done = f32[2,8,6144]{2,0,1:T(2,128)S(1)} async-done(((f32[2,8,6144]{2,0,1:T(2,128)}), f32[2,8,6144]{2,0,1:T(2,128)S(1)}, u32[]{:S(2)}, u32[]{:S(2)}) %all-to-all-start) | async-done | bytes 393248 | tf_op jit(solution)/shard_map/all_to_all | solution.py:28
  55.8 0.5 fusion
  56.3 0.2 convolution_bitcast_fusion
  56.5 0.9 copy.16
  57.4 3.6 %all-to-all-start.1 = ((f32[1,8,6144]{2,0,1:T(1,128)}), f32[1,8,6144]{2,0,1:T(1,128)S(1)}, u32[]{:S(2)}, u32[]{:S(2)}) async-start(f32[1,8,6144]{2,0,1:T(1,128)} %copy.16), calls=%async_computation.2 | async-start | bytes 393216 | tf_op jit(solution)/shard_map/all_to_all | solution.py:47
  61.1 0.7 gather_fusion
  61.7 0.1 gather.14
  61.8 7.0 %all-to-all-done.1 = f32[1,8,6144]{2,0,1:T(1,128)S(1)} async-done(((f32[1,8,6144]{2,0,1:T(1,128)}), f32[1,8,6144]{2,0,1:T(1,128)S(1)}, u32[]{:S(2)}, u32[]{:S(2)}) %all-to-all-start.1) | async-done | bytes 196640 | tf_op jit(solution)/shard_map/all_to_all | solution.py:47
  68.8 0.5 reduce
  69.4 0.4 copy-done.3
  69.8 0.5 copy-done.1
  70.3 0.1 copy-done.2
  70.4 0.9 fusion.8
  71.3 0.5 broadcast.113
  71.8 1.2 %reduce.1 = bf16[8,6144]{1,0:T(8,128)(2,1)S(1)} reduce(bf16[8,1,6144]{2,1,0:T(2,128)(2,1)S(1)} %bitcast.25, bf16[]{:T(256)} %broadcast.113), dimensions={1}, to_apply=%bitcast.19.reduce_sub_computation | reduce | bytes 196610
  73.0 0.7 reshape.168
  73.7 3.4 %all-to-all-start.2 = ((bf16[8,2,3072]{2,1,0:T(2,128)(2,1)}), bf16[8,2,3072]{2,1,0:T(2,128)(2,1)S(1)}, u32[]{:S(2)}, u32[]{:S(2)}) async-start(bf16[8,2,3072]{2,1,0:T(2,128)(2,1)} %reshape.168), calls=%async_computation.3 | async-start | bytes 196608 | tf_op jit(solution)/shard_map/all_to_all | solution.py:55
  77.1 0.1 copy.17
  77.2 6.9 %all-to-all-done.2 = bf16[8,2,3072]{2,1,0:T(2,128)(2,1)S(1)} async-done(((bf16[8,2,3072]{2,1,0:T(2,128)(2,1)}), bf16[8,2,3072]{2,1,0:T(2,128)(2,1)S(1)}, u32[]{:S(2)}, u32[]{:S(2)}) %all-to-all-start.2) | async-done | bytes 98336 | tf_op jit(solution)/shard_map/all_to_all | solution.py:55
  84.3 0.7 gather_fusion.1
  85.0 0.3 broadcast_select_fusion
  85.2 10.2 %all_to_all.24 = bf16[2,8,6144]{2,0,1:T(2,128)(2,1)S(1)} all-to-all(bf16[2,8,6144]{2,0,1:T(2,128)(2,1)S(1)} %broadcast_select_fusion), channel_id=1, replica_groups=mesh['expert'=8,'dp'=4] {'expert'}, dimensions={1} | all-to-all | bytes 393216 | tf_op jit(solution)/shard_map/all_to_all | solution.py:60
  95.5 0.8 reshape.147
  (18 shorter events, 0.4 us)
Async XLA Ops:
  7.2 29.3 %reduce-scatter.2.cloned.1.call-start = ((), (), s32[]{:S(2)}) async-start(), calls=%async_computation.5 | async-start | bytes 983040 | tf_op jit(solution)/shard_map/reduce_scatter | solution.py:25
  38.6 17.2 %all-to-all-start = ((f32[2,8,6144]{2,0,1:T(2,128)}), f32[2,8,6144]{2,0,1:T(2,128)S(1)}, u32[]{:S(2)}, u32[]{:S(2)}) async-start(f32[2,8,6144]{2,0,1:T(2,128)} %copy.14), calls=%async_computation.1 | async-start | bytes 786432 | tf_op jit(solution)/shard_map/all_to_all | solution.py:28
  44.1 0.7 copy-start.4
  44.9 0.7 copy-start.5
  45.6 10.7 %copy-start = (s32[8]{0:T(128)S(1)}, s32[8]{0:T(128)}, u32[]{:S(2)}) copy-start(s32[8]{0:T(128)} %param.13) | copy-start | bytes 100
  57.4 11.4 %all-to-all-start.1 = ((f32[1,8,6144]{2,0,1:T(1,128)}), f32[1,8,6144]{2,0,1:T(1,128)S(1)}, u32[]{:S(2)}, u32[]{:S(2)}) async-start(f32[1,8,6144]{2,0,1:T(1,128)} %copy.16), calls=%async_computation.2 | async-start | bytes 393216 | tf_op jit(solution)/shard_map/all_to_all | solution.py:47
  68.8 0.9 copy-start.3
  69.3 1.0 copy-start.1
  69.3 1.0 %copy-start.2 = (f32[1,32,1536]{2,1,0:T(8,128)S(1)}, f32[1,32,1536]{2,1,0:T(8,128)}, u32[]{:S(2)}) copy-start(f32[1,32,1536]{2,1,0:T(8,128)} %param.9) | copy-start | bytes 589828
  73.7 10.4 %all-to-all-start.2 = ((bf16[8,2,3072]{2,1,0:T(2,128)(2,1)}), bf16[8,2,3072]{2,1,0:T(2,128)(2,1)S(1)}, u32[]{:S(2)}, u32[]{:S(2)}) async-start(bf16[8,2,3072]{2,1,0:T(2,128)(2,1)} %reshape.168), calls=%async_computation.3 | async-start | bytes 196608 | tf_op jit(solution)/shard_map/all_to_all | solution.py:55
Sparse Core Ops, SparseCore 0:
  10.5 25.9 reduce-scatter.1
where the time goes:
time: 104 us; the launch traced here: 103 us
  waiting for transfers between devices  53.4 us (51%)
  between operations  14.2 us (14%)
  starting transfers between devices  12.5 us (12%)
  blocking collectives  10.2 us (10%)
  local copies, waits for them, and re-layouts  9.29 us (9%)
  other arithmetic  2.86 us (3%)
    reduce_scatter x1, waiting for transfers between devices, on_device(): lax.psum_scatter(grads[0].astype(jnp.float32).astype(jnp.bfloat16), 'dp',...  28.6 us
    all_to_all x1, blocking collectives, on_device(): lax.all_to_all(outbound, 'expert', split_axis=1, concat_axis=1, tiled=True)  10.2 us
    all_to_all x1, waiting for transfers between devices, on_device(): lax.all_to_all(summed.reshape(slot_count, device_count, piece_size), 'exp...  10.2 us
    all_to_all x1, waiting for transfers between devices, on_device(): lax.all_to_all(outgoing, 'expert', split_axis=1, concat_axis=1, tiled=True)  7.03 us
    all_to_all x1, waiting for transfers between devices, on_device(): lax.all_to_all(fresh, 'expert', split_axis=1, concat_axis=0, tiled=True)  6.95 us
    all_to_all x1, starting transfers between devices, on_device(): lax.all_to_all(summed.reshape(slot_count, device_count, piece_size), 'exp...  5.52 us
    unnamed x16, local copies, waits for them, and re-layouts  3.66 us
    all_to_all x1, starting transfers between devices, on_device(): lax.all_to_all(outgoing, 'expert', split_axis=1, concat_axis=1, tiled=True)  3.62 us
  transfers between devices with their start and end apart: 4, of which 4 were waited for; matrix products, arithmetic and copies ran while one was open for 1% of the time, Pallas kernels for 0%

commit v1 on v0

--- a/solution.py
+++ b/solution.py
@@ -1,6 +1,10 @@
+import functools
+
 import jax
 import jax.numpy as jnp
 from jax import lax
+from jax.experimental import pallas as pl
+from jax.experimental.pallas import tpu as pltpu
 from jax.sharding import PartitionSpec as P
 
 beta_first = 0.9
@@ -10,9 +14,321 @@
 epsilon = 1e-08
 scale_first = 1.0 - 0.9**40
 scale_second = 1.0 - 0.999**40
-
-
-def on_device(grads, master, moment, second, old_place, new_place, owner_slot):
+MESH = pl.DeviceIdType.MESH
+F32 = jnp.float32
+BF16 = jnp.bfloat16
+TILE = 16
+
+
+def adam(master, moment, second, grad):
+    new_moment = beta_first * moment + (1.0 - beta_first) * grad
+    new_second = beta_second * second + (1.0 - beta_second) * grad * grad
+    update = new_moment / scale_first / (jnp.sqrt(new_second / scale_second) + epsilon)
+    new_master = master - learn_rate * (update + weight_decay * master)
+    return new_master, new_moment, new_second
+
+
+def piece_at(j, width):
+    rows = pl.ds(pl.multiple_of(((j // 2) % 2) * TILE, TILE), TILE)
+    cols = pl.ds(pl.multiple_of(((j // 4) * 2 + j % 2) * width, 128), width)
+    return rows, cols
+
+
+def kernel(
+    n,
+    grads,
+    master,
+    moment,
+    second,
+    old_place,
+    new_place,
+    owner_slot,
+    slot_grad,
+    replicas,
+    own,
+    core_in,
+    cross_out,
+    cross_in,
+    summed,
+    incoming,
+    acc,
+    to_owner,
+    state,
+    state_out,
+    pieces_in,
+    fresh,
+    outbound,
+    load_sem,
+    core_sem,
+    cross_sem,
+    part_send,
+    part_recv,
+    state_send,
+    state_recv,
+    owner_send,
+    owner_recv,
+    fresh_send,
+    fresh_recv,
+):
+    me = lax.axis_index("expert")
+    dp = lax.axis_index("dp")
+    x, core = dp // 2, dp % 2
+    near = x * 2 + (1 - core)
+    far = (1 - x) * 2 + core
+    quarter = master.shape[1]
+    width = grads.shape[3] * 2 // n
+    chunks = [(r, a) for r in range(2) for a in range(2)]
+
+    def rows_of(dp_at, a=0, size=quarter):
+        return pl.ds(pl.multiple_of(dp_at * quarter + a * TILE, TILE), size)
+
+    loads = [
+        pltpu.make_async_copy(src.at[0], state.at[i], load_sem.at[i])
+        for i, src in enumerate((master, moment, second))
+    ]
+    loads += [
+        pltpu.make_async_copy(
+            grads.at[0, :, rows_of((1 - x) * 2 + core)], own.at[0], load_sem.at[3]
+        ),
+        pltpu.make_async_copy(grads.at[0, :, rows_of(dp)], own.at[1], load_sem.at[4]),
+    ]
+    for load in loads:
+        load.start()
+
+    barrier = pltpu.get_barrier_semaphore()
+    for d in range(1, n):
+        pl.semaphore_signal(
+            barrier, inc=1, device_id={"expert": lax.rem(me + d, n)}, device_id_type=MESH
+        )
+    for other in (near, far):
+        pl.semaphore_signal(barrier, inc=1, device_id={"dp": other}, device_id_type=MESH)
+    pl.semaphore_wait(barrier, n + 1)
+
+    core_copies = []
+    for half, x_at in ((0, 1 - x), (1, x)):
+        for t, (r, a) in enumerate(chunks):
+            copy = pltpu.make_async_remote_copy(
+                src_ref=grads.at[0, r, rows_of(x_at * 2 + (1 - core), a, TILE)],
+                dst_ref=core_in.at[half, r, pl.ds(a * TILE, TILE)],
+                send_sem=core_sem.at[0, half, t],
+                recv_sem=core_sem.at[1, half, t],
+                device_id={"dp": near},
+                device_id_type=MESH,
+            )
+            copy.start()
+            core_copies.append(copy)
+
+    for load in loads[:3]:
+        load.wait()
+    state_out[...] = state[...].astype(BF16)
+    state_copies = []
+    for d in range(1, n):
+        j = lax.rem(me + d, n)
+        rows, cols = piece_at(j, width)
+        copy = pltpu.make_async_remote_copy(
+            src_ref=state_out.at[:, rows, cols],
+            dst_ref=pieces_in.at[me],
+            send_sem=state_send.at[d],
+            recv_sem=state_recv.at[me],
+            device_id={"expert": j},
+            device_id_type=MESH,
+        )
+        copy.start()
+        state_copies.append(copy)
+    my_rows, my_cols = piece_at(me, width)
+    pltpu.make_async_copy(
+        state_out.at[:, my_rows, my_cols], pieces_in.at[me], state_recv.at[me]
+    ).start()
+
+    loads[3].wait()
+    cross_copies = []
+    for t, (r, a) in enumerate(chunks):
+        core_copies[t].wait_recv()
+        at = pl.ds(a * TILE, TILE)
+        cross_out[r, at] = (own[0, r, at].astype(F32) + core_in[0, r, at].astype(F32)).astype(BF16)
+        copy = pltpu.make_async_remote_copy(
+            src_ref=cross_out.at[r, at],
+            dst_ref=cross_in.at[r, at],
+            send_sem=cross_sem.at[0, t],
+            recv_sem=cross_sem.at[1, t],
+            device_id={"dp": far},
+            device_id_type=MESH,
+        )
+        copy.start()
+        cross_copies.append(copy)
+
+    loads[4].wait()
+    for t, (r, a) in enumerate(chunks):
+        core_copies[4 + t].wait_recv()
+        cross_copies[t].wait_recv()
+        at = pl.ds(a * TILE, TILE)
+        summed[r, at] = (
+            own[1, r, at].astype(F32)
+            + core_in[1, r, at].astype(F32)
+            + cross_in[r, at].astype(F32)
+        ).astype(BF16)
+        for high in range(2):
+            for side in range(2):
+                j = 4 * ((me // 4 + 1 + high) % 2) + 2 * a + (me % 2 + side) % 2
+                rows, cols = piece_at(j, width)
+
+                @pl.when(j != me)
+                def _():
+                    pltpu.make_async_remote_copy(
+                        src_ref=summed.at[r, at, cols],
+                        dst_ref=incoming.at[me, r],
+                        send_sem=part_send.at[j, r],
+                        recv_sem=part_recv.at[me, r],
+                        device_id={"expert": j},
+                        device_id_type=MESH,
+                    ).start()
+
+                @pl.when(j == me)
+                def _():
+                    pltpu.make_async_copy(
+                        summed.at[r, at, cols], incoming.at[me, r], part_recv.at[me, r]
+                    ).start()
+
+    holds = [
+        [owner_slot[old_place[e, r]] for e in range(n)] for r in range(2)
+    ]
+
+    def sum_of(r, k):
+        total = None
+        for e in range(n):
+            weight = jnp.where(holds[r][e] == k, 1.0, 0.0).astype(F32)
+            term = weight * incoming[e, r].astype(F32)
+            total = term if total is None else total + term
+        return total
+
+    def wait_parts(r):
+        for e in range(n):
+            pltpu.make_async_copy(incoming.at[e, r], incoming.at[e, r], part_recv.at[e, r]).wait()
+
+    wait_parts(0)
+
+    @pl.loop(0, n)
+    def _(k):
+        acc[k] = sum_of(0, k)
+
+    wait_parts(1)
+
+    @pl.loop(0, n)
+    def _(d):
+        k = lax.rem(me + d + 1, n)
+        acc[k] = acc[k] + sum_of(1, k)
+        to_owner[k] = acc[k].astype(BF16)
+
+        @pl.when(k != me)
+        def _():
+            pltpu.make_async_remote_copy(
+                src_ref=to_owner.at[k],
+                dst_ref=slot_grad.at[my_rows, my_cols],
+                send_sem=owner_send.at[k],
+                recv_sem=owner_recv.at[me],
+                device_id={"expert": k},
+                device_id_type=MESH,
+            ).start()
+
+        @pl.when(k == me)
+        def _():
+            pltpu.make_async_copy(
+                to_owner.at[k], slot_grad.at[my_rows, my_cols], owner_recv.at[me]
+            ).start()
+
+    for e in range(n):
+        pltpu.make_async_copy(pieces_in.at[e], pieces_in.at[e], state_recv.at[e]).wait()
+
+    @pl.loop(0, n)
+    def _(k):
+        fresh[k] = adam(
+            pieces_in[k, 0].astype(F32),
+            pieces_in[k, 1].astype(F32),
+            pieces_in[k, 2].astype(F32),
+            acc[k],
+        )[0].astype(BF16)
+
+    for d in range(1, n + 1):
+        j = lax.rem(me + d, n)
+        for r in range(2):
+            outbound[j, r] = fresh[owner_slot[new_place[j, r]]]
+        if d < n:
+            pltpu.make_async_remote_copy(
+                src_ref=outbound.at[j],
+                dst_ref=replicas.at[:, my_rows, my_cols],
+                send_sem=fresh_send.at[j],
+                recv_sem=fresh_recv.at[me],
+                device_id={"expert": j},
+                device_id_type=MESH,
+            ).start()
+        else:
+            pltpu.make_async_copy(
+                outbound.at[j], replicas.at[:, my_rows, my_cols], fresh_recv.at[me]
+            ).start()
+
+    for e in range(n):
+        rows, cols = piece_at(e, width)
+        pltpu.make_async_copy(to_owner.at[e], slot_grad.at[rows, cols], owner_recv.at[e]).wait()
+        pltpu.make_async_copy(outbound.at[e], replicas.at[:, rows, cols], fresh_recv.at[e]).wait()
+    for copy in core_copies + state_copies + cross_copies:
+        copy.wait_send()
+    for d in range(1, n):
+        j = lax.rem(me + d, n)
+        for r in range(2):
+            pltpu.make_async_copy(incoming.at[j, r], incoming.at[j, r], part_send.at[j, r]).wait()
+        pltpu.make_async_copy(to_owner.at[j], to_owner.at[j], owner_send.at[j]).wait()
+        pltpu.make_async_copy(outbound.at[j], outbound.at[j], fresh_send.at[j]).wait()
+
+
+def by_kernel(grads, master, moment, second, old_place, new_place, owner_slot):
+    n = lax.axis_size("expert")
+    quarter, cols = master.shape[1:]
+    width = cols * 2 // n
+    dma = pltpu.SemaphoreType.DMA
+    any_spec = pl.BlockSpec(memory_space=pl.ANY)
+    smem_spec = pl.BlockSpec(memory_space=pltpu.SMEM)
+    slot_grad, replicas = pl.pallas_call(
+        functools.partial(kernel, n),
+        out_shape=(
+            jax.ShapeDtypeStruct((quarter, cols), BF16),
+            jax.ShapeDtypeStruct((2, quarter, cols), BF16),
+        ),
+        in_specs=[any_spec] * 4 + [smem_spec] * 3,
+        out_specs=(any_spec, any_spec),
+        scratch_shapes=[
+            pltpu.VMEM((2, 2, quarter, cols), BF16),
+            pltpu.VMEM((2, 2, quarter, cols), BF16),
+            pltpu.VMEM((2, quarter, cols), BF16),
+            pltpu.VMEM((2, quarter, cols), BF16),
+            pltpu.VMEM((2, quarter, cols), BF16),
+            pltpu.VMEM((n, 2, TILE, width), BF16),
+            pltpu.VMEM((n, TILE, width), F32),
+            pltpu.VMEM((n, TILE, width), BF16),
+            pltpu.VMEM((3, quarter, cols), F32),
+            pltpu.VMEM((3, quarter, cols), BF16),
+            pltpu.VMEM((n, 3, TILE, width), BF16),
+            pltpu.VMEM((n, TILE, width), BF16),
+            pltpu.VMEM((n, 2, TILE, width), BF16),
+            dma((5,)),
+            dma((2, 2, 4)),
+            dma((2, 4)),
+            dma((n, 2)),
+            dma((n, 2)),
+            dma((n,)),
+            dma((n,)),
+            dma((n,)),
+            dma((n,)),
+            dma((n,)),
+            dma((n,)),
+        ],
+        compiler_params=pltpu.CompilerParams(collective_id=0, has_side_effects=True),
+        name="reduce_update_refresh",
+    )(grads, master, moment, second, old_place, new_place, owner_slot)
+    new_master, new_moment, new_second = adam(master, moment, second, slot_grad[None].astype(F32))
+    return (new_master, new_moment, new_second, replicas)
+
+
+def by_collectives(grads, master, moment, second, old_place, new_place, owner_slot):
     device_count = lax.axis_size("expert")
     slot_count = grads.shape[1]
     col_count = grads.shape[3]
@@ -47,10 +363,7 @@
     slot_grad = lax.all_to_all(outgoing, "expert", split_axis=1, concat_axis=1, tiled=True).reshape(
         own_count, quarter_rows, col_count
     )
-    new_moment = beta_first * moment + (1.0 - beta_first) * slot_grad
-    new_second = beta_second * second + (1.0 - beta_second) * slot_grad * slot_grad
-    update = new_moment / scale_first / (jnp.sqrt(new_second / scale_second) + epsilon)
-    new_master = master - learn_rate * (update + weight_decay * master)
+    new_master, new_moment, new_second = adam(master, moment, second, slot_grad)
     fresh = new_master.astype(jnp.bfloat16).reshape(own_count, device_count, piece_size)
     every_slot = lax.all_to_all(fresh, "expert", split_axis=1, concat_axis=0, tiled=True).reshape(
         device_count * own_count, piece_size
@@ -60,6 +373,20 @@
     received = lax.all_to_all(outbound, "expert", split_axis=1, concat_axis=1, tiled=True)
     replicas = received.reshape(slot_count, quarter_rows, col_count)
     return (new_master, new_moment, new_second, replicas)
+
+
+def on_device(grads, master, moment, second, old_place, new_place, owner_slot):
+    fits = (
+        lax.axis_size("dp") == 4
+        and lax.axis_size("expert") == 8
+        and grads.shape[1] == 2
+        and master.shape[0] == 1
+        and owner_slot.shape[0] == 8
+        and master.shape[1] == 2 * TILE
+        and grads.shape[3] % (4 * 128) == 0
+    )
+    plan = by_kernel if fits else by_collectives
+    return plan(grads, master, moment, second, old_place, new_place, owner_slot)
 
 
 def solution(mesh):

time: 104 us -> 32 us (0.31)
  waiting for transfers between devices: 53.4 us -> 0 us
  Pallas kernels: 0 us -> 26.6 us
  between operations: 14.2 us -> 0.68 us
  starting transfers between devices: 12.5 us -> 0 us
  blocking collectives: 10.2 us -> 0 us
  local copies, waits for them, and re-layouts: 9.29 us -> 2.72 us
    reduce_scatter x1 -> x0, waiting for transfers between devices: 28.6 us -> none  [on_device(): lax.psum_scatter(grads[0].astype(jnp.float32).astype(jnp.bfloat16), 'dp',...]
    pallas_call x0 -> x1, Pallas kernels: none -> 26.6 us  [by_kernel(): pl.pallas_call(functools.partial(kernel, n), out_shape=(jax.ShapeDtypeStr...]
    all_to_all x3 -> x0, waiting for transfers between devices: 24.1 us -> none  [the longest x1 10.2 us: on_device(): lax.all_to_all(summed.reshape(slot_count, device_count, piece_size), 'exp...]
    all_to_all x3 -> x0, starting transfers between devices: 12.5 us -> none  [the longest x1 5.52 us: on_device(): lax.all_to_all(summed.reshape(slot_count, device_count, piece_size), 'exp...]
    all_to_all x1 -> x0, blocking collectives: 10.2 us -> none  [on_device(): lax.all_to_all(outbound, 'expert', split_axis=1, concat_axis=1, tiled=True)]
    reshape x6 -> x0, local copies, waits for them, and re-layouts: 3.11 us -> none  [the longest x2 2.1 us: on_device(): summed.reshape(slot_count, device_count, piece_size)]
    sub x0 -> x1, other arithmetic: none -> 1.83 us  [adam(): new_master = master - learn_rate * (update + weight_decay * master)]
    gather x3 -> x0, local copies, waits for them, and re-layouts: 1.4 us -> none  [the longest x2 0.74 us: on_device(): wanted = owner_slot[new_place.T.reshape(-1)]]
  transfers between devices with their start and end apart: 4 -> 0, of which waited for: 4 -> 0; matrix products, arithmetic and copies ran while one was open for 1% -> 0% of each run, Pallas kernels for 0% -> 0%
where the time goes in v1:
time: 32 us; the launch traced here: 31.9 us
  Pallas kernels  26.6 us (83%)
  local copies, waits for them, and re-layouts  2.72 us (8%)
  other arithmetic  1.83 us (6%)
  between operations  0.68 us (2%)
    pallas_call x1, Pallas kernels, by_kernel(): pl.pallas_call(functools.partial(kernel, n), out_shape=(jax.ShapeDtypeStr...  26.6 us
    unnamed x13, local copies, waits for them, and re-layouts  2.72 us
    sub x1, other arithmetic, adam(): new_master = master - learn_rate * (update + weight_decay * master)  1.83 us

profile of v1, /device:TPU:0, one launch (start us, length us, event | category | flops | bytes accessed | tf_op | source)
XLA Modules:
  0.0 31.9 jit_solution(17042056458385757635)
XLA Ops:
  0.6 0.0 copy-start.4
  0.6 1.4 %copy.11.old_place = s32[8,2]{1,0:T(8,128)} copy(s32[8,2]{0,1:T(2,128)} %param.11) | data formatting | bytes 128 | tf_op args[4]
  2.0 0.0 copy-done.4
  2.0 0.7 %copy.12.new_place = s32[8,2]{1,0:T(8,128)} copy(s32[8,2]{0,1:T(2,128)S(1)} %copy-done.4) | data formatting | bytes 128 | tf_op args[5]
  2.7 0.0 copy-start
  2.7 0.0 copy-start.1
  2.7 0.0 copy-start.2
  2.7 26.6 %reduce_update_refresh.1 = (bf16[32,1536]{1,0:T(8,128)(2,1)}, bf16[2,32,1536]{2,1,0:T(8,128)(2,1)}) custom-call(bf16[1,2,128,1536]{3,2,1,0:T(8,128)(2,1)} %grads.1, f32[1,32,1536]{2,1,0:T(8,128)} %master.1, f32[1,32,1536]{2,1,0:T(8,128)} %moment.1, f32[1,32,1536]{2,1,0:T(8,128)} %second.1, s32[8,2]{1,0:T(8,128)} %copy.11.old_place, s32[8,2]{1,0:T(8,128)} %copy.12.new_place, ...), custom_call_target="tpu_custom_call" | custom-call | tf_op jit(solution)/shard_map/reduce_update_refresh/pallas_call | solution.py:290
  29.3 0.0 copy-done
  29.3 0.0 copy-done.1
  29.3 0.0 copy-done.2
  29.3 0.0 copy-start.3
  29.4 1.8 %multiply_subtract_fusion = (f32[1,32,1536]{2,1,0:T(8,128)}, f32[1,32,1536]{2,1,0:T(8,128)}, f32[1,32,1536]{2,1,0:T(8,128)}) fusion(f32[1,32,1536]{2,1,0:T(8,128)S(1)} %copy-done, bf16[32,1536]{1,0:T(8,128)(2,1)} %get-tuple-element.6, f32[1,32,1536]{2,1,0:T(8,128)S(1)} %copy-done.1, f32[1,32,1536]{2,1,0:T(8,128)S(1)} %copy-done.2), kind=kLoop, calls=%fused_computation.6 | loop fusion | flops 786432 | bytes 1277952 | tf_op jit(solution)/shard_map/sub | solution.py:27
  31.2 0.0 copy-done.3
  31.2 0.7 %copy.14 = bf16[2,32,1536]{2,1,0:T(8,128)(2,1)} copy(bf16[2,32,1536]{2,1,0:T(8,128)(2,1)S(1)} %copy-done.3) | data formatting | bytes 393216
Async XLA Ops:
  0.6 1.4 %copy-start.4 = (s32[8,2]{0,1:T(2,128)S(1)}, s32[8,2]{0,1:T(2,128)}, u32[]{:S(2)}) copy-start(s32[8,2]{0,1:T(2,128)} %param.12) | copy-start | bytes 196
  2.7 26.6 %copy-start = (f32[1,32,1536]{2,1,0:T(8,128)S(1)}, f32[1,32,1536]{2,1,0:T(8,128)}, u32[]{:S(2)}) copy-start(f32[1,32,1536]{2,1,0:T(8,128)} %master.1) | copy-start | bytes 589828
  2.7 26.7 %copy-start.1 = (f32[1,32,1536]{2,1,0:T(8,128)S(1)}, f32[1,32,1536]{2,1,0:T(8,128)}, u32[]{:S(2)}) copy-start(f32[1,32,1536]{2,1,0:T(8,128)} %moment.1) | copy-start | bytes 589828
  2.7 26.7 %copy-start.2 = (f32[1,32,1536]{2,1,0:T(8,128)S(1)}, f32[1,32,1536]{2,1,0:T(8,128)}, u32[]{:S(2)}) copy-start(f32[1,32,1536]{2,1,0:T(8,128)} %second.1) | copy-start | bytes 589828
  29.3 1.8 %copy-start.3 = (bf16[2,32,1536]{2,1,0:T(8,128)(2,1)S(1)}, bf16[2,32,1536]{2,1,0:T(8,128)(2,1)}, u32[]{:S(2)}) copy-start(bf16[2,32,1536]{2,1,0:T(8,128)(2,1)} %get-tuple-element.18) | copy-start | bytes 589828

commit v2 on v1

--- a/solution.py
+++ b/solution.py
@@ -122,23 +122,34 @@
         load.wait()
     state_out[...] = state[...].astype(BF16)
     state_copies = []
-    for d in range(1, n):
-        j = lax.rem(me + d, n)
-        rows, cols = piece_at(j, width)
-        copy = pltpu.make_async_remote_copy(
-            src_ref=state_out.at[:, rows, cols],
-            dst_ref=pieces_in.at[me],
-            send_sem=state_send.at[d],
-            recv_sem=state_recv.at[me],
-            device_id={"expert": j},
-            device_id_type=MESH,
-        )
-        copy.start()
-        state_copies.append(copy)
     my_rows, my_cols = piece_at(me, width)
-    pltpu.make_async_copy(
-        state_out.at[:, my_rows, my_cols], pieces_in.at[me], state_recv.at[me]
-    ).start()
+
+    def send_state(first, count):
+        part = pl.ds(first, count)
+        for d in range(1, n):
+            j = lax.rem(me + d, n)
+            rows, cols = piece_at(j, width)
+            copy = pltpu.make_async_remote_copy(
+                src_ref=state_out.at[part, rows, cols],
+                dst_ref=pieces_in.at[me, part],
+                send_sem=state_send.at[d, first],
+                recv_sem=state_recv.at[me, first],
+                device_id={"expert": j},
+                device_id_type=MESH,
+            )
+            copy.start()
+            state_copies.append(copy)
+        pltpu.make_async_copy(
+            state_out.at[part, my_rows, my_cols], pieces_in.at[me, part], state_recv.at[me, first]
+        ).start()
+
+    def wait_state(first, count):
+        part = pl.ds(first, count)
+        for e in range(n):
+            piece = pieces_in.at[e, part]
+            pltpu.make_async_copy(piece, piece, state_recv.at[e, first]).wait()
+
+    send_state(0, 2)
 
     loads[3].wait()
     cross_copies = []
@@ -189,8 +200,10 @@
                         summed.at[r, at, cols], incoming.at[me, r], part_recv.at[me, r]
                     ).start()
 
+    send_state(2, 1)
+
     holds = [
-        [owner_slot[old_place[e, r]] for e in range(n)] for r in range(2)
+        [owner_slot[old_place[r, e]] for e in range(n)] for r in range(2)
     ]
 
     def sum_of(r, k):
@@ -236,8 +249,8 @@
                 to_owner.at[k], slot_grad.at[my_rows, my_cols], owner_recv.at[me]
             ).start()
 
-    for e in range(n):
-        pltpu.make_async_copy(pieces_in.at[e], pieces_in.at[e], state_recv.at[e]).wait()
+    wait_state(0, 2)
+    wait_state(2, 1)
 
     @pl.loop(0, n)
     def _(k):
@@ -251,7 +264,7 @@
     for d in range(1, n + 1):
         j = lax.rem(me + d, n)
         for r in range(2):
-            outbound[j, r] = fresh[owner_slot[new_place[j, r]]]
+            outbound[j, r] = fresh[owner_slot[new_place[r, j]]]
         if d < n:
             pltpu.make_async_remote_copy(
                 src_ref=outbound.at[j],
@@ -314,8 +327,8 @@
             dma((2, 4)),
             dma((n, 2)),
             dma((n, 2)),
-            dma((n,)),
-            dma((n,)),
+            dma((n, 3)),
+            dma((n, 3)),
             dma((n,)),
             dma((n,)),
             dma((n,)),
@@ -323,7 +336,7 @@
         ],
         compiler_params=pltpu.CompilerParams(collective_id=0, has_side_effects=True),
         name="reduce_update_refresh",
-    )(grads, master, moment, second, old_place, new_place, owner_slot)
+    )(grads, master, moment, second, old_place.T, new_place.T, owner_slot)
     new_master, new_moment, new_second = adam(master, moment, second, slot_grad[None].astype(F32))
     return (new_master, new_moment, new_second, replicas)
 

time: 32 us -> 30.5 us (0.953)
  local copies, waits for them, and re-layouts: 2.72 us -> 0.69 us
  Pallas kernels: 26.6 us -> 27.1 us
    unnamed x13 -> x9, local copies, waits for them, and re-layouts: 2.72 us -> 0.69 us
    pallas_call x1, Pallas kernels: 26.6 us -> 27.1 us  [by_kernel(): pl.pallas_call(functools.partial(kernel, n), out_shape=(jax.ShapeDtypeStr...]
where the time goes in v2:
time: 30.5 us; the launch traced here: 30.3 us
  Pallas kernels  27.1 us (89%)
  other arithmetic  1.83 us (6%)
  between operations  0.7 us (2%)
  local copies, waits for them, and re-layouts  0.69 us (2%)
    pallas_call x1, Pallas kernels, by_kernel(): pl.pallas_call(functools.partial(kernel, n), out_shape=(jax.ShapeDtypeStr...  27.1 us
    sub x1, other arithmetic, adam(): new_master = master - learn_rate * (update + weight_decay * master)  1.83 us
    unnamed x9, local copies, waits for them, and re-layouts  0.69 us

profile of v2, /device:TPU:0, one launch (start us, length us, event | category | flops | bytes accessed | tf_op | source)
XLA Modules:
  0.0 30.3 jit_solution(14808202025179478524)
XLA Ops:
  0.6 0.0 copy-start
  0.6 0.0 copy-start.1
  0.7 0.0 copy-start.2
  0.7 27.1 %reduce_update_refresh.1 = (bf16[32,1536]{1,0:T(8,128)(2,1)}, bf16[2,32,1536]{2,1,0:T(8,128)(2,1)}) custom-call(bf16[1,2,128,1536]{3,2,1,0:T(8,128)(2,1)} %grads.1, f32[1,32,1536]{2,1,0:T(8,128)} %master.1, f32[1,32,1536]{2,1,0:T(8,128)} %moment.1, f32[1,32,1536]{2,1,0:T(8,128)} %second.1, s32[2,8]{1,0:T(2,128)} %bitcast.12, s32[2,8]{1,0:T(2,128)} %bitcast.13, ...), custom_call_target="tpu_custom_call" | custom-call | tf_op jit(solution)/shard_map/reduce_update_refresh/pallas_call | solution.py:303
  27.8 0.0 copy-done
  27.8 0.0 copy-done.1
  27.8 0.0 copy-done.2
  27.8 0.0 copy-start.3
  27.8 1.8 %multiply_subtract_fusion = (f32[1,32,1536]{2,1,0:T(8,128)}, f32[1,32,1536]{2,1,0:T(8,128)}, f32[1,32,1536]{2,1,0:T(8,128)}) fusion(f32[1,32,1536]{2,1,0:T(8,128)S(1)} %copy-done, bf16[32,1536]{1,0:T(8,128)(2,1)} %get-tuple-element.6, f32[1,32,1536]{2,1,0:T(8,128)S(1)} %copy-done.1, f32[1,32,1536]{2,1,0:T(8,128)S(1)} %copy-done.2), kind=kLoop, calls=%fused_computation.6 | loop fusion | flops 786432 | bytes 1277952 | tf_op jit(solution)/shard_map/sub | solution.py:27
  29.6 0.0 copy-done.3
  29.6 0.7 %copy.12 = bf16[2,32,1536]{2,1,0:T(8,128)(2,1)} copy(bf16[2,32,1536]{2,1,0:T(8,128)(2,1)S(1)} %copy-done.3) | data formatting | bytes 393216
Async XLA Ops:
  0.6 27.1 %copy-start = (f32[1,32,1536]{2,1,0:T(8,128)S(1)}, f32[1,32,1536]{2,1,0:T(8,128)}, u32[]{:S(2)}) copy-start(f32[1,32,1536]{2,1,0:T(8,128)} %master.1) | copy-start | bytes 589828
  0.6 27.1 %copy-start.1 = (f32[1,32,1536]{2,1,0:T(8,128)S(1)}, f32[1,32,1536]{2,1,0:T(8,128)}, u32[]{:S(2)}) copy-start(f32[1,32,1536]{2,1,0:T(8,128)} %moment.1) | copy-start | bytes 589828
  0.7 27.1 %copy-start.2 = (f32[1,32,1536]{2,1,0:T(8,128)S(1)}, f32[1,32,1536]{2,1,0:T(8,128)}, u32[]{:S(2)}) copy-start(f32[1,32,1536]{2,1,0:T(8,128)} %second.1) | copy-start | bytes 589828
  27.8 1.8 %copy-start.3 = (bf16[2,32,1536]{2,1,0:T(8,128)(2,1)S(1)}, bf16[2,32,1536]{2,1,0:T(8,128)(2,1)}, u32[]{:S(2)}) copy-start(bf16[2,32,1536]{2,1,0:T(8,128)(2,1)} %get-tuple-element.18) | copy-start | bytes 589828

commit v3 on v2

v3 whole, which is shorter than its diff:
```python
import functools

import jax
import jax.numpy as jnp
from jax import lax
from jax.experimental import pallas as pl
from jax.experimental.pallas import tpu as pltpu
from jax.sharding import PartitionSpec as P

beta_first = 0.9
beta_second = 0.999
learn_rate = 0.02
weight_decay = 0.1
epsilon = 1e-08
scale_first = 1.0 - 0.9**40
scale_second = 1.0 - 0.999**40
MESH = pl.DeviceIdType.MESH
F32 = jnp.float32
BF16 = jnp.bfloat16
TILE = 16


def adam(master, moment, second, grad):
    new_moment = beta_first * moment + (1.0 - beta_first) * grad
    new_second = beta_second * second + (1.0 - beta_second) * grad * grad
    update = new_moment / scale_first / (jnp.sqrt(new_second / scale_second) + epsilon)
    new_master = master - learn_rate * (update + weight_decay * master)
    return new_master, new_moment, new_second


def piece_at(j, width):
    rows = pl.ds(pl.multiple_of(((j // 2) % 2) * TILE, TILE), TILE)
    cols = pl.ds(pl.multiple_of(((j // 4) * 2 + j % 2) * width, 128), width)
    return rows, cols


def kernel(
    n,
    grads,
    master,
    moment,
    second,
    old_place,
    new_place,
    owner_slot,
    new_master,
    new_moment,
    new_second,
    replicas,
    own,
    core_in,
    cross_out,
    cross_in,
    summed,
    incoming,
    acc,
    to_owner,
    slot_grad,
    state,
    state_out,
    pieces_in,
    fresh,
    outbound,
    load_sem,
    store_sem,
    core_send,
    core_recv,
    cross_send,
    cross_recv,
    part_send,
    part_recv,
    state_send,
    state_recv,
    owner_sem,
    fresh_sem,
):
    me = lax.axis_index("expert")
    dp = lax.axis_index("dp")
    x, core = dp // 2, dp % 2
    near = x * 2 + (1 - core)
    far = (1 - x) * 2 + core
    quarter = master.shape[1]
    width = grads.shape[3] * 2 // n
    chunks = [(r, a) for r in range(2) for a in range(2)]

    def rows_of(dp_at, a=0, size=quarter):
        return pl.ds(pl.multiple_of(dp_at * quarter + a * TILE, TILE), size)

    def wait_bytes(ref, sem):
        pltpu.make_async_copy(ref, ref, sem).wait()

    def send(src, dst, send_sem, recv_sem, to):
        pltpu.make_async_remote_copy(
            src_ref=src,
            dst_ref=dst,
            send_sem=send_sem,
            recv_sem=recv_sem,
            device_id=to,
            device_id_type=MESH,
        ).start()

    loads = [
        pltpu.make_async_copy(src.at[0], state.at[i], load_sem.at[i])
        for i, src in enumerate((master, moment, second))
    ]
    loads += [
        pltpu.make_async_copy(
            grads.at[0, :, rows_of((1 - x) * 2 + core)], own.at[0], load_sem.at[3]
        ),
        pltpu.make_async_copy(grads.at[0, :, rows_of(dp)], own.at[1], load_sem.at[4]),
    ]
    barrier = pltpu.get_barrier_semaphore()
    for d in range(1, n):
        pl.semaphore_signal(
            barrier, inc=1, device_id={"expert": lax.rem(me + d, n)}, device_id_type=MESH
        )
    for other in (near, far):
        pl.semaphore_signal(barrier, inc=1, device_id={"dp": other}, device_id_type=MESH)
    for load in loads:
        load.start()
    for i in range(3):
        loads[i].wait()
        state_out[i] = state[i].astype(BF16)
    pl.semaphore_wait(barrier, n + 1)

    for half, x_at in ((0, 1 - x), (1, x)):
        for t, (r, a) in enumerate(chunks):
            send(
                grads.at[0, r, rows_of(x_at * 2 + (1 - core), a, TILE)],
                core_in.at[half, r, pl.ds(a * TILE, TILE)],
                core_send,
                core_recv.at[half, t],
                {"dp": near},
            )

    my_rows, my_cols = piece_at(me, width)

    def send_state(first, count):
        part = pl.ds(first, count)
        for d in range(1, n):
            j = lax.rem(me + d, n)
            rows, cols = piece_at(j, width)
            send(
                state_out.at[part, rows, cols],
                pieces_in.at[me, part],
                state_send.at[first],
                state_recv.at[first],
                {"expert": j},
            )
        pltpu.make_async_copy(
            state_out.at[part, my_rows, my_cols], pieces_in.at[me, part], state_recv.at[first]
        ).start()

    send_state(0, 2)

    loads[3].wait()
    for t, (r, a) in enumerate(chunks):
        at = pl.ds(a * TILE, TILE)
        wait_bytes(core_in.at[0, r, at], core_recv.at[0, t])
        cross_out[r, at] = (own[0, r, at].astype(F32) + core_in[0, r, at].astype(F32)).astype(BF16)
        send(cross_out.at[r, at], cross_in.at[r, at], cross_send, cross_recv.at[t], {"dp": far})

    loads[4].wait()
    for t, (r, a) in enumerate(chunks):
        at = pl.ds(a * TILE, TILE)
        wait_bytes(core_in.at[1, r, at], core_recv.at[1, t])
        wait_bytes(cross_in.at[r, at], cross_recv.at[t])
        summed[r, at] = (
            own[1, r, at].astype(F32)
            + core_in[1, r, at].astype(F32)
            + cross_in[r, at].astype(F32)
        ).astype(BF16)
        for high in range(2):
            for side in range(2):
                j = 4 * ((me // 4 + 1 + high) % 2) + 2 * a + (me % 2 + side) % 2
                rows, cols = piece_at(j, width)

                @pl.when(j != me)
                def _():
                    send(
                        summed.at[r, at, cols],
                        incoming.at[r, me],
                        part_send.at[r],
                        part_recv.at[r],
                        {"expert": j},
                    )

                @pl.when(j == me)
                def _():
                    pltpu.make_async_copy(
                        summed.at[r, at, cols], incoming.at[r, me], part_recv.at[r]
                    ).start()

    send_state(2, 1)

    holds = [[owner_slot[old_place[r, e]] for e in range(n)] for r in range(2)]

    def sum_of(r, k):
        total = None
        for e in range(n):
            weight = jnp.where(holds[r][e] == k, 1.0, 0.0).astype(F32)
            term = weight * incoming[r, e].astype(F32)
            total = term if total is None else total + term
        return total

    wait_bytes(incoming.at[0], part_recv.at[0])

    @pl.loop(0, n)
    def _(k):
        acc[k] = sum_of(0, k)

    wait_bytes(incoming.at[1], part_recv.at[1])

    @pl.loop(0, n)
    def _(d):
        k = lax.rem(me + d + 1, n)
        acc[k] = acc[k] + sum_of(1, k)
        to_owner[k] = acc[k].astype(BF16)

        @pl.when(k != me)
        def _():
            send(
                to_owner.at[k],
                slot_grad.at[my_rows, my_cols],
                owner_sem.at[0],
                owner_sem.at[1],
                {"expert": k},
            )

        @pl.when(k == me)
        def _():
            pltpu.make_async_copy(
                to_owner.at[k], slot_grad.at[my_rows, my_cols], owner_sem.at[1]
            ).start()

    wait_bytes(pieces_in.at[:, pl.ds(0, 2)], state_recv.at[0])
    wait_bytes(pieces_in.at[:, pl.ds(2, 1)], state_recv.at[2])

    @pl.loop(0, n)
    def _(k):
        fresh[k] = adam(
            pieces_in[k, 0].astype(F32),
            pieces_in[k, 1].astype(F32),
            pieces_in[k, 2].astype(F32),
            acc[k],
        )[0].astype(BF16)

    for d in range(1, n + 1):
        j = lax.rem(me + d, n)
        for r in range(2):
            outbound[j, r] = fresh[owner_slot[new_place[r, j]]]
        there = replicas.at[:, my_rows, my_cols]
        if d < n:
            send(outbound.at[j], there, fresh_sem.at[0], fresh_sem.at[1], {"expert": j})
        else:
            pltpu.make_async_copy(outbound.at[j], there, fresh_sem.at[1]).start()

    wait_bytes(slot_grad, owner_sem.at[1])

    @pl.loop(0, n)
    def _(e):
        rows, cols = piece_at(e, width)
        result = adam(
            state[0, rows, cols],
            state[1, rows, cols],
            state[2, rows, cols],
            slot_grad[rows, cols].astype(F32),
        )
        for i in range(3):
            state[i, rows, cols] = result[i]

    stores = [
        pltpu.make_async_copy(state.at[i], dst.at[0], store_sem.at[i])
        for i, dst in enumerate((new_master, new_moment, new_second))
    ]
    for store in stores:
        store.start()

    others = pl.ds(0, n - 1)
    wait_bytes(own, core_send)
    wait_bytes(cross_out, cross_send)
    wait_bytes(pieces_in.at[others, pl.ds(0, 2)], state_send.at[0])
    wait_bytes(pieces_in.at[others, pl.ds(2, 1)], state_send.at[2])
    for r in range(2):
        wait_bytes(incoming.at[r, others], part_send.at[r])
    wait_bytes(to_owner.at[others], owner_sem.at[0])
    for store in stores:
        store.wait()
    wait_bytes(outbound.at[others], fresh_sem.at[0])
    wait_bytes(replicas, fresh_sem.at[1])


def hand_over(*refs):
    count = len(refs) // 2
    copies = [
        pltpu.make_async_copy(refs[i], refs[count + i], refs[-1].at[i]) for i in range(count)
    ]
    for copy in copies:
        copy.start()
    for copy in copies:
        copy.wait()


def by_kernel(grads, master, moment, second, old_place, new_place, owner_slot):
    n = lax.axis_size("expert")
    quarter, cols = master.shape[1:]
    width = cols * 2 // n
    dma = pltpu.SemaphoreType.DMA
    any_spec = pl.BlockSpec(memory_space=pl.ANY)
    smem_spec = pl.BlockSpec(memory_space=pltpu.SMEM)
    out_shape = (jax.ShapeDtypeStruct(master.shape, F32),) * 3 + (
        jax.ShapeDtypeStruct((2, quarter, cols), BF16),
    )
    results = pl.pallas_call(
        functools.partial(kernel, n),
        out_shape=out_shape,
        in_specs=[any_spec] * 4 + [smem_spec] * 3,
        out_specs=(any_spec,) * 4,
        scratch_shapes=[
            pltpu.VMEM((2, 2, quarter, cols), BF16),
            pltpu.VMEM((2, 2, quarter, cols), BF16),
            pltpu.VMEM((2, quarter, cols), BF16),
            pltpu.VMEM((2, quarter, cols), BF16),
            pltpu.VMEM((2, quarter, cols), BF16),
            pltpu.VMEM((2, n, TILE, width), BF16),
            pltpu.VMEM((n, TILE, width), F32),
            pltpu.VMEM((n, TILE, width), BF16),
            pltpu.VMEM((quarter, cols), BF16),
            pltpu.VMEM((3, quarter, cols), F32),
            pltpu.VMEM((3, quarter, cols), BF16),
            pltpu.VMEM((n, 3, TILE, width), BF16),
            pltpu.VMEM((n, TILE, width), BF16),
            pltpu.VMEM((n, 2, TILE, width), BF16),
            dma((5,)),
            dma((3,)),
            dma,
            dma((2, 4)),
            dma,
            dma((4,)),
            dma((2,)),
            dma((2,)),
            dma((3,)),
            dma((3,)),
            dma((2,)),
            dma((2,)),
        ],
        compiler_params=pltpu.CompilerParams(collective_id=0, has_side_effects=True),
        name="reduce_update_refresh",
    )(grads, master, moment, second, old_place.T, new_place.T, owner_slot)
    return pl.pallas_call(
        hand_over,
        out_shape=out_shape,
        in_specs=[any_spec] * 4,
        out_specs=(any_spec,) * 4,
        scratch_shapes=[dma((4,))],
        name="hand_over",
    )(*results)


def by_collectives(grads, master, moment, second, old_place, new_place, owner_slot):
    device_count = lax.axis_size("expert")
    slot_count = grads.shape[1]
    col_count = grads.shape[3]
    own_count = master.shape[0]
    quarter_rows = master.shape[1]
    piece_size = quarter_rows * col_count // device_count
    expert_count = owner_slot.shape[0]
    expert_ids = jnp.arange(expert_count, dtype=jnp.int32)
    old_hot = (expert_ids[:, None] == old_place.T.reshape(-1)[None, :]).astype(jnp.float32)
    summed = lax.psum_scatter(
        grads[0].astype(jnp.float32).astype(jnp.bfloat16), "dp", scatter_dimension=1, tiled=True
    ).astype(jnp.float32)
    incoming = lax.all_to_all(
        summed.reshape(slot_count, device_count, piece_size),
        "expert",
        split_axis=1,
        concat_axis=1,
        tiled=True,
    )
    expert_part = jnp.dot(
        old_hot,
        incoming.reshape(slot_count * device_count, piece_size),
        precision=lax.Precision.HIGHEST,
    )
    slot_ids = jnp.arange(device_count * own_count, dtype=jnp.int32)
    owner_hot = (
        (slot_ids[:, None] == owner_slot[None, :])
        .astype(jnp.float32)
        .reshape(device_count, own_count, expert_count)
    )
    outgoing = jnp.einsum("koe,ep->okp", owner_hot, expert_part, precision=lax.Precision.HIGHEST)
    slot_grad = lax.all_to_all(outgoing, "expert", split_axis=1, concat_axis=1, tiled=True).reshape(
        own_count, quarter_rows, col_count
    )
    new_master, new_moment, new_second = adam(master, moment, second, slot_grad)
    fresh = new_master.astype(jnp.bfloat16).reshape(own_count, device_count, piece_size)
    every_slot = lax.all_to_all(fresh, "expert", split_axis=1, concat_axis=0, tiled=True).reshape(
        device_count * own_count, piece_size
    )
    wanted = owner_slot[new_place.T.reshape(-1)]
    outbound = jnp.take(every_slot, wanted, axis=0).reshape(slot_count, device_count, piece_size)
    received = lax.all_to_all(outbound, "expert", split_axis=1, concat_axis=1, tiled=True)
    replicas = received.reshape(slot_count, quarter_rows, col_count)
    return (new_master, new_moment, new_second, replicas)


def on_device(grads, master, moment, second, old_place, new_place, owner_slot):
    fits = (
        lax.axis_size("dp") == 4
        and lax.axis_size("expert") == 8
        and grads.shape[1] == 2
        and master.shape[0] == 1
        and owner_slot.shape[0] == 8
        and master.shape[1] == 2 * TILE
        and grads.shape[3] % (4 * 128) == 0
    )
    plan = by_kernel if fits else by_collectives
    return plan(grads, master, moment, second, old_place, new_place, owner_slot)


def solution(mesh):
    placed = (
        P("dp", "expert", None, None),
        P("expert", "dp", None),
        P("expert", "dp", None),
        P("expert", "dp", None),
        P(),
        P(),
        P(),
    )
    return jax.shard_map(
        on_device,
        mesh=mesh,
        in_specs=placed,
        out_specs=(
            P("expert", "dp", None),
            P("expert", "dp", None),
            P("expert", "dp", None),
            P("expert", "dp", None),
        ),
        check_vma=False,
    )
```

time: 30.5 us -> 51.7 us (1.70)
  Pallas kernels: 27.1 us -> 50.9 us
  other arithmetic: 1.83 us -> 0 us
  local copies, waits for them, and re-layouts: 0.69 us -> 0 us
    pallas_call x1 -> x2, Pallas kernels: 27.1 us -> 50.9 us  [the longest x1 25.9 us: by_kernel(): pl.pallas_call(functools.partial(kernel, n), out_shape=out_shape, in_spec...]
    sub x1 -> x0, other arithmetic: 1.83 us -> none  [adam(): new_master = master - learn_rate * (update + weight_decay * master)]
    unnamed x9 -> x0, local copies, waits for them, and re-layouts: 0.69 us -> none
where the time goes in v3:
time: 51.7 us; the launch traced here: 51.5 us
  Pallas kernels  50.9 us (98%)
  between operations  0.64 us (1%)
    pallas_call x1, Pallas kernels, by_kernel(): pl.pallas_call(functools.partial(kernel, n), out_shape=out_shape, in_spec...  25.9 us
    pallas_call x1, Pallas kernels, by_kernel(): pl.pallas_call(hand_over, out_shape=out_shape, in_specs=[any_spec] * 4, o...  25 us

profile of v3, /device:TPU:0, one launch (start us, length us, event | category | flops | bytes accessed | tf_op | source)
XLA Modules:
  0.0 51.5 jit_solution(473765383557425182)
XLA Ops:
  0.6 25.9 %reduce_update_refresh.1 = (f32[1,32,1536]{2,1,0:T(8,128)}, f32[1,32,1536]{2,1,0:T(8,128)}, f32[1,32,1536]{2,1,0:T(8,128)}, bf16[2,32,1536]{2,1,0:T(8,128)(2,1)}) custom-call(bf16[1,2,128,1536]{3,2,1,0:T(8,128)(2,1)} %grads.1, f32[1,32,1536]{2,1,0:T(8,128)} %master.1, f32[1,32,1536]{2,1,0:T(8,128)} %moment.1, f32[1,32,1536]{2,1,0:T(8,128)} %second.1, ...), custom_call_target="tpu_custom_call" | custom-call | tf_op jit(solution)/shard_map/reduce_update_refresh/pallas_call | solution.py:314
  26.6 25.0 %hand_over.1 = (f32[1,32,1536]{2,1,0:T(8,128)}, f32[1,32,1536]{2,1,0:T(8,128)}, f32[1,32,1536]{2,1,0:T(8,128)}, bf16[2,32,1536]{2,1,0:T(8,128)(2,1)}) custom-call(f32[1,32,1536]{2,1,0:T(8,128)} %get-tuple-element.8.refs_0_, f32[1,32,1536]{2,1,0:T(8,128)} %get-tuple-element.9.refs_1_, f32[1,32,1536]{2,1,0:T(8,128)} %get-tuple-element.10.refs_2_, ...), custom_call_target="tpu_custom_call" | custom-call | tf_op jit(solution)/shard_map/hand_over/pallas_call | solution.py:350

commit v4 on v3

--- a/solution.py
+++ b/solution.py
@@ -62,7 +62,6 @@
     fresh,
     outbound,
     load_sem,
-    store_sem,
     core_send,
     core_recv,
     cross_send,
@@ -266,15 +265,8 @@
             state[2, rows, cols],
             slot_grad[rows, cols].astype(F32),
         )
-        for i in range(3):
-            state[i, rows, cols] = result[i]
-
-    stores = [
-        pltpu.make_async_copy(state.at[i], dst.at[0], store_sem.at[i])
-        for i, dst in enumerate((new_master, new_moment, new_second))
-    ]
-    for store in stores:
-        store.start()
+        for i, out in enumerate((new_master, new_moment, new_second)):
+            out[0, rows, cols] = result[i]
 
     others = pl.ds(0, n - 1)
     wait_bytes(own, core_send)
@@ -284,8 +276,6 @@
     for r in range(2):
         wait_bytes(incoming.at[r, others], part_send.at[r])
     wait_bytes(to_owner.at[others], owner_sem.at[0])
-    for store in stores:
-        store.wait()
     wait_bytes(outbound.at[others], fresh_sem.at[0])
     wait_bytes(replicas, fresh_sem.at[1])
 
@@ -311,11 +301,12 @@
     out_shape = (jax.ShapeDtypeStruct(master.shape, F32),) * 3 + (
         jax.ShapeDtypeStruct((2, quarter, cols), BF16),
     )
+    vmem_spec = pl.BlockSpec(memory_space=pltpu.VMEM)
     results = pl.pallas_call(
         functools.partial(kernel, n),
-        out_shape=out_shape,
+        out_shape=tuple(pltpu.VMEM(out.shape, out.dtype) for out in out_shape),
         in_specs=[any_spec] * 4 + [smem_spec] * 3,
-        out_specs=(any_spec,) * 4,
+        out_specs=(vmem_spec,) * 4,
         scratch_shapes=[
             pltpu.VMEM((2, 2, quarter, cols), BF16),
             pltpu.VMEM((2, 2, quarter, cols), BF16),
@@ -332,7 +323,6 @@
             pltpu.VMEM((n, TILE, width), BF16),
             pltpu.VMEM((n, 2, TILE, width), BF16),
             dma((5,)),
-            dma((3,)),
             dma,
             dma((2, 4)),
             dma,
@@ -350,7 +340,7 @@
     return pl.pallas_call(
         hand_over,
         out_shape=out_shape,
-        in_specs=[any_spec] * 4,
+        in_specs=[vmem_spec] * 4,
         out_specs=(any_spec,) * 4,
         scratch_shapes=[dma((4,))],
         name="hand_over",

time: 51.7 us -> 31.5 us (0.61)
  Pallas kernels: 50.9 us -> 27.9 us
  local copies, waits for them, and re-layouts: 0 us -> 2.71 us
    pallas_call x2, Pallas kernels: 50.9 us -> 27.9 us  [the longest x1 25.8 us: by_kernel(): pl.pallas_call(functools.partial(kernel, n), out_shape=tuple((pltpu.VMEM(...]
    unnamed x0 -> x8, local copies, waits for them, and re-layouts: none -> 2.71 us
where the time goes in v4:
time: 31.5 us; the launch traced here: 31.3 us
  Pallas kernels  27.9 us (89%)
  local copies, waits for them, and re-layouts  2.71 us (9%)
  between operations  0.65 us (2%)
    pallas_call x1, Pallas kernels, by_kernel(): pl.pallas_call(functools.partial(kernel, n), out_shape=tuple((pltpu.VMEM(...  25.8 us
    unnamed x8, local copies, waits for them, and re-layouts  2.71 us
    pallas_call x1, Pallas kernels, by_kernel(): pl.pallas_call(hand_over, out_shape=out_shape, in_specs=[vmem_spec] * 4,...  2.12 us

profile of v4, /device:TPU:0, one launch (start us, length us, event | category | flops | bytes accessed | tf_op | source)
XLA Modules:
  0.0 31.3 jit_solution(4987254913261602639)
XLA Ops:
  0.6 25.8 %reduce_update_refresh.1 = (f32[1,32,1536]{2,1,0:T(8,128)S(1)}, f32[1,32,1536]{2,1,0:T(8,128)S(1)}, f32[1,32,1536]{2,1,0:T(8,128)S(1)}, bf16[2,32,1536]{2,1,0:T(8,128)(2,1)S(1)}) custom-call(bf16[1,2,128,1536]{3,2,1,0:T(8,128)(2,1)} %grads.1, f32[1,32,1536]{2,1,0:T(8,128)} %master.1, f32[1,32,1536]{2,1,0:T(8,128)} %moment.1, f32[1,32,1536]{2,1,0:T(8,128)} %second.1, ...), custom_call_target="tpu_custom_call" | custom-call | tf_op jit(solution)/shard_map/reduce_update_refresh/pallas_call | solution.py:305
  26.4 0.0 copy-start
  26.4 0.7 %copy-done = f32[1,32,1536]{2,1,0:T(8,128)} copy-done((f32[1,32,1536]{2,1,0:T(8,128)}, f32[1,32,1536]{2,1,0:T(8,128)S(1)}, u32[]{:S(2)}) %copy-start) | copy-done | bytes 196632
  27.1 0.0 copy-start.1
  27.1 0.7 %copy-done.1 = f32[1,32,1536]{2,1,0:T(8,128)} copy-done((f32[1,32,1536]{2,1,0:T(8,128)}, f32[1,32,1536]{2,1,0:T(8,128)S(1)}, u32[]{:S(2)}) %copy-start.1) | copy-done | bytes 196632
  27.8 0.0 copy-start.2
  27.8 0.7 %copy-done.2 = f32[1,32,1536]{2,1,0:T(8,128)} copy-done((f32[1,32,1536]{2,1,0:T(8,128)}, f32[1,32,1536]{2,1,0:T(8,128)S(1)}, u32[]{:S(2)}) %copy-start.2) | copy-done | bytes 196632
  28.5 0.0 copy-start.3
  28.5 0.7 %copy-done.3 = bf16[2,32,1536]{2,1,0:T(8,128)(2,1)} copy-done((bf16[2,32,1536]{2,1,0:T(8,128)(2,1)}, bf16[2,32,1536]{2,1,0:T(8,128)(2,1)S(1)}, u32[]{:S(2)}) %copy-start.3) | copy-done | bytes 196632
  29.2 2.1 %hand_over.1 = (f32[1,32,1536]{2,1,0:T(8,128)}, f32[1,32,1536]{2,1,0:T(8,128)}, f32[1,32,1536]{2,1,0:T(8,128)}, bf16[2,32,1536]{2,1,0:T(8,128)(2,1)}) custom-call(f32[1,32,1536]{2,1,0:T(8,128)} %copy-done, f32[1,32,1536]{2,1,0:T(8,128)} %copy-done.1, f32[1,32,1536]{2,1,0:T(8,128)} %copy-done.2, bf16[2,32,1536]{2,1,0:T(8,128)(2,1)} %copy-done.3), custom_call_target="tpu_custom_call" | custom-call | tf_op jit(solution)/shard_map/hand_over/pallas_call | solution.py:340
Async XLA Ops:
  26.4 0.7 %copy-start = (f32[1,32,1536]{2,1,0:T(8,128)}, f32[1,32,1536]{2,1,0:T(8,128)S(1)}, u32[]{:S(2)}) copy-start(f32[1,32,1536]{2,1,0:T(8,128)S(1)} %get-tuple-element.8.refs_0_) | copy-start | bytes 589828
  27.1 0.7 %copy-start.1 = (f32[1,32,1536]{2,1,0:T(8,128)}, f32[1,32,1536]{2,1,0:T(8,128)S(1)}, u32[]{:S(2)}) copy-start(f32[1,32,1536]{2,1,0:T(8,128)S(1)} %get-tuple-element.9.refs_1_) | copy-start | bytes 589828
  27.8 0.7 %copy-start.2 = (f32[1,32,1536]{2,1,0:T(8,128)}, f32[1,32,1536]{2,1,0:T(8,128)S(1)}, u32[]{:S(2)}) copy-start(f32[1,32,1536]{2,1,0:T(8,128)S(1)} %get-tuple-element.10.refs_2_) | copy-start | bytes 589828
  28.5 0.7 %copy-start.3 = (bf16[2,32,1536]{2,1,0:T(8,128)(2,1)}, bf16[2,32,1536]{2,1,0:T(8,128)(2,1)S(1)}, u32[]{:S(2)}) copy-start(bf16[2,32,1536]{2,1,0:T(8,128)(2,1)S(1)} %get-tuple-element.11.refs_3_) | copy-start | bytes 589828

commit v5 on v4

--- a/solution.py
+++ b/solution.py
@@ -340,11 +340,12 @@
     return pl.pallas_call(
         hand_over,
         out_shape=out_shape,
-        in_specs=[vmem_spec] * 4,
+        in_specs=[any_spec] * 4,
         out_specs=(any_spec,) * 4,
         scratch_shapes=[dma((4,))],
+        compiler_params=pltpu.CompilerParams(vmem_limit_bytes=1 << 20),
         name="hand_over",
-    )(*results)
+    )(*[pltpu.with_memory_space_constraint(result, pltpu.VMEM) for result in results])
 
 
 def by_collectives(grads, master, moment, second, old_place, new_place, owner_slot):

time: 31.5 us -> 27.5 us (0.87)
  local copies, waits for them, and re-layouts: 2.71 us -> 0 us
  Pallas kernels: 27.9 us -> 26.7 us
    unnamed x8 -> x0, local copies, waits for them, and re-layouts: 2.71 us -> none
    pallas_call x1, Pallas kernels: 2.12 us -> 0.91 us  [by_kernel(): pl.pallas_call(hand_over, out_shape=out_shape, in_specs=[any_spec] * 4, o...]
where the time goes in v5:
time: 27.5 us; the launch traced here: 27.3 us
  Pallas kernels  26.7 us (97%)
  between operations  0.64 us (2%)
    pallas_call x1, Pallas kernels, by_kernel(): pl.pallas_call(functools.partial(kernel, n), out_shape=tuple((pltpu.VMEM(...  25.8 us
    pallas_call x1, Pallas kernels, by_kernel(): pl.pallas_call(hand_over, out_shape=out_shape, in_specs=[any_spec] * 4, o...  0.91 us

profile of v5, /device:TPU:0, one launch (start us, length us, event | category | flops | bytes accessed | tf_op | source)
XLA Modules:
  0.0 27.3 jit_solution(1228706811129672229)
XLA Ops:
  0.6 25.8 %reduce_update_refresh.1 = (f32[1,32,1536]{2,1,0:T(8,128)S(1)}, f32[1,32,1536]{2,1,0:T(8,128)S(1)}, f32[1,32,1536]{2,1,0:T(8,128)S(1)}, bf16[2,32,1536]{2,1,0:T(8,128)(2,1)S(1)}) custom-call(bf16[1,2,128,1536]{3,2,1,0:T(8,128)(2,1)} %grads.1, f32[1,32,1536]{2,1,0:T(8,128)} %master.1, f32[1,32,1536]{2,1,0:T(8,128)} %moment.1, f32[1,32,1536]{2,1,0:T(8,128)} %second.1, ...), custom_call_target="tpu_custom_call" | custom-call | tf_op jit(solution)/shard_map/reduce_update_refresh/pallas_call | solution.py:305
  26.4 0.9 %hand_over.1 = (f32[1,32,1536]{2,1,0:T(8,128)}, f32[1,32,1536]{2,1,0:T(8,128)}, f32[1,32,1536]{2,1,0:T(8,128)}, bf16[2,32,1536]{2,1,0:T(8,128)(2,1)}) custom-call(f32[1,32,1536]{2,1,0:T(8,128)S(1)} %get-tuple-element.8.refs_0_, f32[1,32,1536]{2,1,0:T(8,128)S(1)} %get-tuple-element.9.refs_1_, f32[1,32,1536]{2,1,0:T(8,128)S(1)} %get-tuple-element.10.refs_2_, ...), custom_call_target="tpu_custom_call" | custom-call | tf_op jit(solution)/shard_map/hand_over/pallas_call | solution.py:340

commit v6 on v5

--- a/solution.py
+++ b/solution.py
@@ -18,6 +18,7 @@
 F32 = jnp.float32
 BF16 = jnp.bfloat16
 TILE = 16
+LANES = 128
 
 
 def adam(master, moment, second, grad):
@@ -28,10 +29,10 @@
     return new_master, new_moment, new_second
 
 
-def piece_at(j, width):
+def piece_at(j, n, cols, c):
     rows = pl.ds(pl.multiple_of(((j // 2) % 2) * TILE, TILE), TILE)
-    cols = pl.ds(pl.multiple_of(((j // 4) * 2 + j % 2) * width, 128), width)
-    return rows, cols
+    start = c * (n // 2 * LANES) + ((j // 4) * 2 + j % 2) * LANES
+    return rows, pl.ds(pl.multiple_of(start, LANES), LANES)
 
 
 def kernel(
@@ -53,7 +54,6 @@
     cross_in,
     summed,
     incoming,
-    acc,
     to_owner,
     slot_grad,
     state,
@@ -79,11 +79,12 @@
     near = x * 2 + (1 - core)
     far = (1 - x) * 2 + core
     quarter = master.shape[1]
-    width = grads.shape[3] * 2 // n
-    chunks = [(r, a) for r in range(2) for a in range(2)]
-
-    def rows_of(dp_at, a=0, size=quarter):
-        return pl.ds(pl.multiple_of(dp_at * quarter + a * TILE, TILE), size)
+    width = grads.shape[3]
+    span = n // 2 * LANES
+    chunks = width // span
+
+    def rows_of(dp_at):
+        return pl.ds(pl.multiple_of(dp_at * quarter, TILE), quarter)
 
     def wait_bytes(ref, sem):
         pltpu.make_async_copy(ref, ref, sem).wait()
@@ -119,146 +120,120 @@
         load.start()
     for i in range(3):
         loads[i].wait()
-        state_out[i] = state[i].astype(BF16)
+        for j in range(n):
+            for c in range(chunks):
+                rows, cols = piece_at(j, n, width, c)
+                state_out[j, i, :, c * LANES : (c + 1) * LANES] = state[i, rows, cols].astype(BF16)
     pl.semaphore_wait(barrier, n + 1)
 
     for half, x_at in ((0, 1 - x), (1, x)):
-        for t, (r, a) in enumerate(chunks):
+        for c in range(chunks):
+            at = pl.ds(c * span, span)
             send(
-                grads.at[0, r, rows_of(x_at * 2 + (1 - core), a, TILE)],
-                core_in.at[half, r, pl.ds(a * TILE, TILE)],
+                grads.at[0, :, rows_of(x_at * 2 + (1 - core)), at],
+                core_in.at[half, :, :, at],
                 core_send,
-                core_recv.at[half, t],
+                core_recv.at[half, c],
                 {"dp": near},
             )
 
-    my_rows, my_cols = piece_at(me, width)
-
-    def send_state(first, count):
-        part = pl.ds(first, count)
-        for d in range(1, n):
+    for d in range(1, n):
+        j = lax.rem(me + d, n)
+        send(state_out.at[j], pieces_in.at[me], state_send, state_recv, {"expert": j})
+    pltpu.make_async_copy(state_out.at[me], pieces_in.at[me], state_recv).start()
+
+    loads[3].wait()
+    for c in range(chunks):
+        at = pl.ds(c * span, span)
+        wait_bytes(core_in.at[0, :, :, at], core_recv.at[0, c])
+        cross_out[:, :, at] = (
+            own[0, :, :, at].astype(F32) + core_in[0, :, :, at].astype(F32)
+        ).astype(BF16)
+        send(
+            cross_out.at[:, :, at],
+            cross_in.at[:, :, at],
+            cross_send,
+            cross_recv.at[c],
+            {"dp": far},
+        )
+    loads[4].wait()
+
+    def exchange(c):
+        at = pl.ds(c * span, span)
+        wait_bytes(core_in.at[1, :, :, at], core_recv.at[1, c])
+        wait_bytes(cross_in.at[:, :, at], cross_recv.at[c])
+        summed[:, :, at] = (
+            own[1, :, :, at].astype(F32)
+            + core_in[1, :, :, at].astype(F32)
+            + cross_in[:, :, at].astype(F32)
+        ).astype(BF16)
+        for d in range(1, n + 1):
             j = lax.rem(me + d, n)
-            rows, cols = piece_at(j, width)
-            send(
-                state_out.at[part, rows, cols],
-                pieces_in.at[me, part],
-                state_send.at[first],
-                state_recv.at[first],
-                {"expert": j},
-            )
-        pltpu.make_async_copy(
-            state_out.at[part, my_rows, my_cols], pieces_in.at[me, part], state_recv.at[first]
-        ).start()
-
-    send_state(0, 2)
-
-    loads[3].wait()
-    for t, (r, a) in enumerate(chunks):
-        at = pl.ds(a * TILE, TILE)
-        wait_bytes(core_in.at[0, r, at], core_recv.at[0, t])
-        cross_out[r, at] = (own[0, r, at].astype(F32) + core_in[0, r, at].astype(F32)).astype(BF16)
-        send(cross_out.at[r, at], cross_in.at[r, at], cross_send, cross_recv.at[t], {"dp": far})
-
-    loads[4].wait()
-    for t, (r, a) in enumerate(chunks):
-        at = pl.ds(a * TILE, TILE)
-        wait_bytes(core_in.at[1, r, at], core_recv.at[1, t])
-        wait_bytes(cross_in.at[r, at], cross_recv.at[t])
-        summed[r, at] = (
-            own[1, r, at].astype(F32)
-            + core_in[1, r, at].astype(F32)
-            + cross_in[r, at].astype(F32)
-        ).astype(BF16)
-        for high in range(2):
-            for side in range(2):
-                j = 4 * ((me // 4 + 1 + high) % 2) + 2 * a + (me % 2 + side) % 2
-                rows, cols = piece_at(j, width)
-
-                @pl.when(j != me)
-                def _():
-                    send(
-                        summed.at[r, at, cols],
-                        incoming.at[r, me],
-                        part_send.at[r],
-                        part_recv.at[r],
-                        {"expert": j},
-                    )
-
-                @pl.when(j == me)
-                def _():
-                    pltpu.make_async_copy(
-                        summed.at[r, at, cols], incoming.at[r, me], part_recv.at[r]
-                    ).start()
-
-    send_state(2, 1)
+            rows, cols = piece_at(j, n, width, c)
+            src, dst = summed.at[:, rows, cols], incoming.at[c, me]
+            if d < n:
+                send(src, dst, part_send, part_recv.at[c], {"expert": j})
+            else:
+                pltpu.make_async_copy(src, dst, part_recv.at[c]).start()
 
     holds = [[owner_slot[old_place[r, e]] for e in range(n)] for r in range(2)]
 
-    def sum_of(r, k):
-        total = None
-        for e in range(n):
-            weight = jnp.where(holds[r][e] == k, 1.0, 0.0).astype(F32)
-            term = weight * incoming[r, e].astype(F32)
-            total = term if total is None else total + term
-        return total
-
-    wait_bytes(incoming.at[0], part_recv.at[0])
-
-    @pl.loop(0, n)
-    def _(k):
-        acc[k] = sum_of(0, k)
-
-    wait_bytes(incoming.at[1], part_recv.at[1])
-
-    @pl.loop(0, n)
-    def _(d):
-        k = lax.rem(me + d + 1, n)
-        acc[k] = acc[k] + sum_of(1, k)
-        to_owner[k] = acc[k].astype(BF16)
-
-        @pl.when(k != me)
-        def _():
-            send(
-                to_owner.at[k],
-                slot_grad.at[my_rows, my_cols],
-                owner_sem.at[0],
-                owner_sem.at[1],
-                {"expert": k},
-            )
-
-        @pl.when(k == me)
-        def _():
-            pltpu.make_async_copy(
-                to_owner.at[k], slot_grad.at[my_rows, my_cols], owner_sem.at[1]
-            ).start()
-
-    wait_bytes(pieces_in.at[:, pl.ds(0, 2)], state_recv.at[0])
-    wait_bytes(pieces_in.at[:, pl.ds(2, 1)], state_recv.at[2])
-
-    @pl.loop(0, n)
-    def _(k):
-        fresh[k] = adam(
-            pieces_in[k, 0].astype(F32),
-            pieces_in[k, 1].astype(F32),
-            pieces_in[k, 2].astype(F32),
-            acc[k],
-        )[0].astype(BF16)
-
-    for d in range(1, n + 1):
-        j = lax.rem(me + d, n)
-        for r in range(2):
-            outbound[j, r] = fresh[owner_slot[new_place[r, j]]]
-        there = replicas.at[:, my_rows, my_cols]
-        if d < n:
-            send(outbound.at[j], there, fresh_sem.at[0], fresh_sem.at[1], {"expert": j})
-        else:
-            pltpu.make_async_copy(outbound.at[j], there, fresh_sem.at[1]).start()
+    def update(c):
+        my_rows, my_cols = piece_at(me, n, width, c)
+        lanes = pl.ds(c * LANES, LANES)
+        wait_bytes(incoming.at[c], part_recv.at[c])
+        if c == 0:
+            wait_bytes(pieces_in, state_recv)
+
+        @pl.loop(0, n)
+        def _(d):
+            k = lax.rem(me + d + 1, n)
+            total = None
+            for r in range(2):
+                for e in range(n):
+                    weight = jnp.where(holds[r][e] == k, 1.0, 0.0).astype(F32)
+                    term = weight * incoming[c, e, r].astype(F32)
+                    total = term if total is None else total + term
+            to_owner[c, k] = total.astype(BF16)
+            there = slot_grad.at[my_rows, my_cols]
+
+            @pl.when(k != me)
+            def _():
+                send(to_owner.at[c, k], there, owner_sem.at[0], owner_sem.at[1], {"expert": k})
+
+            @pl.when(k == me)
+            def _():
+                pltpu.make_async_copy(to_owner.at[c, k], there, owner_sem.at[1]).start()
+
+            fresh[k] = adam(
+                pieces_in[k, 0, :, lanes].astype(F32),
+                pieces_in[k, 1, :, lanes].astype(F32),
+                pieces_in[k, 2, :, lanes].astype(F32),
+                total,
+            )[0].astype(BF16)
+
+        for d in range(1, n + 1):
+            j = lax.rem(me + d, n)
+            for r in range(2):
+                outbound[c, j, r] = fresh[owner_slot[new_place[r, j]]]
+            there = replicas.at[:, my_rows, my_cols]
+            if d < n:
+                send(outbound.at[c, j], there, fresh_sem.at[0], fresh_sem.at[1], {"expert": j})
+            else:
+                pltpu.make_async_copy(outbound.at[c, j], there, fresh_sem.at[1]).start()
+
+    exchange(0)
+    for c in range(1, chunks):
+        exchange(c)
+        update(c - 1)
+    update(chunks - 1)
 
     wait_bytes(slot_grad, owner_sem.at[1])
 
     @pl.loop(0, n)
     def _(e):
-        rows, cols = piece_at(e, width)
+        rows = pl.ds(pl.multiple_of((e % 2) * TILE, TILE), TILE)
+        cols = pl.ds(pl.multiple_of((e // 2) * (2 * width // n), LANES), 2 * width // n)
         result = adam(
             state[0, rows, cols],
             state[1, rows, cols],
@@ -271,12 +246,10 @@
     others = pl.ds(0, n - 1)
     wait_bytes(own, core_send)
     wait_bytes(cross_out, cross_send)
-    wait_bytes(pieces_in.at[others, pl.ds(0, 2)], state_send.at[0])
-    wait_bytes(pieces_in.at[others, pl.ds(2, 1)], state_send.at[2])
-    for r in range(2):
-        wait_bytes(incoming.at[r, others], part_send.at[r])
-    wait_bytes(to_owner.at[others], owner_sem.at[0])
-    wait_bytes(outbound.at[others], fresh_sem.at[0])
+    wait_bytes(pieces_in.at[others], state_send)
+    wait_bytes(incoming.at[:, others], part_send)
+    wait_bytes(to_owner.at[:, others], owner_sem.at[0])
+    wait_bytes(outbound.at[:, others], fresh_sem.at[0])
     wait_bytes(replicas, fresh_sem.at[1])
 
 
@@ -295,6 +268,7 @@
     n = lax.axis_size("expert")
     quarter, cols = master.shape[1:]
     width = cols * 2 // n
+    chunks = width // LANES
     dma = pltpu.SemaphoreType.DMA
     any_spec = pl.BlockSpec(memory_space=pl.ANY)
     smem_spec = pl.BlockSpec(memory_space=pltpu.SMEM)
@@ -313,24 +287,23 @@
             pltpu.VMEM((2, quarter, cols), BF16),
             pltpu.VMEM((2, quarter, cols), BF16),
             pltpu.VMEM((2, quarter, cols), BF16),
-            pltpu.VMEM((2, n, TILE, width), BF16),
-            pltpu.VMEM((n, TILE, width), F32),
-            pltpu.VMEM((n, TILE, width), BF16),
+            pltpu.VMEM((chunks, n, 2, TILE, LANES), BF16),
+            pltpu.VMEM((chunks, n, TILE, LANES), BF16),
             pltpu.VMEM((quarter, cols), BF16),
             pltpu.VMEM((3, quarter, cols), F32),
-            pltpu.VMEM((3, quarter, cols), BF16),
             pltpu.VMEM((n, 3, TILE, width), BF16),
-            pltpu.VMEM((n, TILE, width), BF16),
-            pltpu.VMEM((n, 2, TILE, width), BF16),
+            pltpu.VMEM((n, 3, TILE, width), BF16),
+            pltpu.VMEM((n, TILE, LANES), BF16),
+            pltpu.VMEM((chunks, n, 2, TILE, LANES), BF16),
             dma((5,)),
             dma,
-            dma((2, 4)),
+            dma((2, chunks)),
             dma,
-            dma((4,)),
-            dma((2,)),
-            dma((2,)),
-            dma((3,)),
-            dma((3,)),
+            dma((chunks,)),
+            dma,
+            dma((chunks,)),
+            dma,
+            dma,
             dma((2,)),
             dma((2,)),
         ],

time: 27.5 us -> 29.8 us (1.084)
  Pallas kernels: 26.7 us -> 29 us
    pallas_call x1, Pallas kernels: 25.8 us -> 28.1 us  [by_kernel(): pl.pallas_call(functools.partial(kernel, n), out_shape=tuple((pltpu.VMEM(...]
where the time goes in v6:
time: 29.8 us; the launch traced here: 29.6 us
  Pallas kernels  29 us (97%)
  between operations  0.64 us (2%)
    pallas_call x1, Pallas kernels, by_kernel(): pl.pallas_call(functools.partial(kernel, n), out_shape=tuple((pltpu.VMEM(...  28.1 us
    pallas_call x1, Pallas kernels, by_kernel(): pl.pallas_call(hand_over, out_shape=out_shape, in_specs=[any_spec] * 4, o...  0.91 us

profile of v6, /device:TPU:0, one launch (start us, length us, event | category | flops | bytes accessed | tf_op | source)
XLA Modules:
  0.0 29.6 jit_solution(5764851492199201972)
XLA Ops:
  0.6 28.1 %reduce_update_refresh.1 = (f32[1,32,1536]{2,1,0:T(8,128)S(1)}, f32[1,32,1536]{2,1,0:T(8,128)S(1)}, f32[1,32,1536]{2,1,0:T(8,128)S(1)}, bf16[2,32,1536]{2,1,0:T(8,128)(2,1)S(1)}) custom-call(bf16[1,2,128,1536]{3,2,1,0:T(8,128)(2,1)} %grads.1, f32[1,32,1536]{2,1,0:T(8,128)} %master.1, f32[1,32,1536]{2,1,0:T(8,128)} %moment.1, f32[1,32,1536]{2,1,0:T(8,128)} %second.1, ...), custom_call_target="tpu_custom_call" | custom-call | tf_op jit(solution)/shard_map/reduce_update_refresh/pallas_call | solution.py:279
  28.7 0.9 %hand_over.1 = (f32[1,32,1536]{2,1,0:T(8,128)}, f32[1,32,1536]{2,1,0:T(8,128)}, f32[1,32,1536]{2,1,0:T(8,128)}, bf16[2,32,1536]{2,1,0:T(8,128)(2,1)}) custom-call(f32[1,32,1536]{2,1,0:T(8,128)S(1)} %get-tuple-element.8.refs_0_, f32[1,32,1536]{2,1,0:T(8,128)S(1)} %get-tuple-element.9.refs_1_, f32[1,32,1536]{2,1,0:T(8,128)S(1)} %get-tuple-element.10.refs_2_, ...), custom_call_target="tpu_custom_call" | custom-call | tf_op jit(solution)/shard_map/hand_over/pallas_call | solution.py:313

commit v7 on v5

--- a/solution.py
+++ b/solution.py
@@ -119,7 +119,9 @@
         load.start()
     for i in range(3):
         loads[i].wait()
-        state_out[i] = state[i].astype(BF16)
+        for j in range(n):
+            rows, cols = piece_at(j, width)
+            state_out[j, i] = state[i, rows, cols].astype(BF16)
     pl.semaphore_wait(barrier, n + 1)
 
     for half, x_at in ((0, 1 - x), (1, x)):
@@ -134,23 +136,10 @@
 
     my_rows, my_cols = piece_at(me, width)
 
-    def send_state(first, count):
-        part = pl.ds(first, count)
-        for d in range(1, n):
-            j = lax.rem(me + d, n)
-            rows, cols = piece_at(j, width)
-            send(
-                state_out.at[part, rows, cols],
-                pieces_in.at[me, part],
-                state_send.at[first],
-                state_recv.at[first],
-                {"expert": j},
-            )
-        pltpu.make_async_copy(
-            state_out.at[part, my_rows, my_cols], pieces_in.at[me, part], state_recv.at[first]
-        ).start()
-
-    send_state(0, 2)
+    for d in range(1, n):
+        j = lax.rem(me + d, n)
+        send(state_out.at[j], pieces_in.at[me], state_send, state_recv, {"expert": j})
+    pltpu.make_async_copy(state_out.at[me], pieces_in.at[me], state_recv).start()
 
     loads[3].wait()
     for t, (r, a) in enumerate(chunks):
@@ -164,20 +153,23 @@
         at = pl.ds(a * TILE, TILE)
         wait_bytes(core_in.at[1, r, at], core_recv.at[1, t])
         wait_bytes(cross_in.at[r, at], cross_recv.at[t])
-        summed[r, at] = (
+        total = (
             own[1, r, at].astype(F32)
             + core_in[1, r, at].astype(F32)
             + cross_in[r, at].astype(F32)
         ).astype(BF16)
+        for j in range(2 * a, n, 4):
+            for j_at in (j, j + 1):
+                b = (j_at // 4) * 2 + j_at % 2
+                summed[r, j_at] = total[:, b * width : (b + 1) * width]
         for high in range(2):
             for side in range(2):
                 j = 4 * ((me // 4 + 1 + high) % 2) + 2 * a + (me % 2 + side) % 2
-                rows, cols = piece_at(j, width)
 
                 @pl.when(j != me)
                 def _():
                     send(
-                        summed.at[r, at, cols],
+                        summed.at[r, j],
                         incoming.at[r, me],
                         part_send.at[r],
                         part_recv.at[r],
@@ -187,10 +179,8 @@
                 @pl.when(j == me)
                 def _():
                     pltpu.make_async_copy(
-                        summed.at[r, at, cols], incoming.at[r, me], part_recv.at[r]
+                        summed.at[r, j], incoming.at[r, me], part_recv.at[r]
                     ).start()
-
-    send_state(2, 1)
 
     holds = [[owner_slot[old_place[r, e]] for e in range(n)] for r in range(2)]
 
@@ -220,7 +210,7 @@
         def _():
             send(
                 to_owner.at[k],
-                slot_grad.at[my_rows, my_cols],
+                slot_grad.at[me],
                 owner_sem.at[0],
                 owner_sem.at[1],
                 {"expert": k},
@@ -229,11 +219,10 @@
         @pl.when(k == me)
         def _():
             pltpu.make_async_copy(
-                to_owner.at[k], slot_grad.at[my_rows, my_cols], owner_sem.at[1]
+                to_owner.at[k], slot_grad.at[me], owner_sem.at[1]
             ).start()
 
-    wait_bytes(pieces_in.at[:, pl.ds(0, 2)], state_recv.at[0])
-    wait_bytes(pieces_in.at[:, pl.ds(2, 1)], state_recv.at[2])
+    wait_bytes(pieces_in, state_recv)
 
     @pl.loop(0, n)
     def _(k):
@@ -263,7 +252,7 @@
             state[0, rows, cols],
             state[1, rows, cols],
             state[2, rows, cols],
-            slot_grad[rows, cols].astype(F32),
+            slot_grad[e].astype(F32),
         )
         for i, out in enumerate((new_master, new_moment, new_second)):
             out[0, rows, cols] = result[i]
@@ -271,8 +260,7 @@
     others = pl.ds(0, n - 1)
     wait_bytes(own, core_send)
     wait_bytes(cross_out, cross_send)
-    wait_bytes(pieces_in.at[others, pl.ds(0, 2)], state_send.at[0])
-    wait_bytes(pieces_in.at[others, pl.ds(2, 1)], state_send.at[2])
+    wait_bytes(pieces_in.at[others], state_send)
     for r in range(2):
         wait_bytes(incoming.at[r, others], part_send.at[r])
     wait_bytes(to_owner.at[others], owner_sem.at[0])
@@ -312,13 +300,13 @@
             pltpu.VMEM((2, 2, quarter, cols), BF16),
             pltpu.VMEM((2, quarter, cols), BF16),
             pltpu.VMEM((2, quarter, cols), BF16),
-            pltpu.VMEM((2, quarter, cols), BF16),
+            pltpu.VMEM((2, n, TILE, width), BF16),
             pltpu.VMEM((2, n, TILE, width), BF16),
             pltpu.VMEM((n, TILE, width), F32),
             pltpu.VMEM((n, TILE, width), BF16),
-            pltpu.VMEM((quarter, cols), BF16),
+            pltpu.VMEM((n, TILE, width), BF16),
             pltpu.VMEM((3, quarter, cols), F32),
-            pltpu.VMEM((3, quarter, cols), BF16),
+            pltpu.VMEM((n, 3, TILE, width), BF16),
             pltpu.VMEM((n, 3, TILE, width), BF16),
             pltpu.VMEM((n, TILE, width), BF16),
             pltpu.VMEM((n, 2, TILE, width), BF16),
@@ -329,8 +317,8 @@
             dma((4,)),
             dma((2,)),
             dma((2,)),
-            dma((3,)),
-            dma((3,)),
+            dma,
+            dma,
             dma((2,)),
             dma((2,)),
         ],

time: 27.5 us -> 27.2 us (0.989)
  Pallas kernels: 26.7 us -> 26.4 us
    pallas_call x1, Pallas kernels: 25.8 us -> 25.5 us  [by_kernel(): pl.pallas_call(functools.partial(kernel, n), out_shape=tuple((pltpu.VMEM(...]
where the time goes in v7:
time: 27.2 us; the launch traced here: 27 us
  Pallas kernels  26.4 us (97%)
  between operations  0.64 us (2%)
    pallas_call x1, Pallas kernels, by_kernel(): pl.pallas_call(functools.partial(kernel, n), out_shape=tuple((pltpu.VMEM(...  25.5 us
    pallas_call x1, Pallas kernels, by_kernel(): pl.pallas_call(hand_over, out_shape=out_shape, in_specs=[any_spec] * 4, o...  0.91 us

profile of v7, /device:TPU:0, one launch (start us, length us, event | category | flops | bytes accessed | tf_op | source)
XLA Modules:
  0.0 27.0 jit_solution(14862065480315050271)
XLA Ops:
  0.6 25.5 %reduce_update_refresh.1 = (f32[1,32,1536]{2,1,0:T(8,128)S(1)}, f32[1,32,1536]{2,1,0:T(8,128)S(1)}, f32[1,32,1536]{2,1,0:T(8,128)S(1)}, bf16[2,32,1536]{2,1,0:T(8,128)(2,1)S(1)}) custom-call(bf16[1,2,128,1536]{3,2,1,0:T(8,128)(2,1)} %grads.1, f32[1,32,1536]{2,1,0:T(8,128)} %master.1, f32[1,32,1536]{2,1,0:T(8,128)} %moment.1, f32[1,32,1536]{2,1,0:T(8,128)} %second.1, ...), custom_call_target="tpu_custom_call" | custom-call | tf_op jit(solution)/shard_map/reduce_update_refresh/pallas_call | solution.py:293
  26.1 0.9 %hand_over.1 = (f32[1,32,1536]{2,1,0:T(8,128)}, f32[1,32,1536]{2,1,0:T(8,128)}, f32[1,32,1536]{2,1,0:T(8,128)}, bf16[2,32,1536]{2,1,0:T(8,128)(2,1)}) custom-call(f32[1,32,1536]{2,1,0:T(8,128)S(1)} %get-tuple-element.8.refs_0_, f32[1,32,1536]{2,1,0:T(8,128)S(1)} %get-tuple-element.9.refs_1_, f32[1,32,1536]{2,1,0:T(8,128)S(1)} %get-tuple-element.10.refs_2_, ...), custom_call_target="tpu_custom_call" | custom-call | tf_op jit(solution)/shard_map/hand_over/pallas_call | solution.py:328

commit v8 on v7

--- a/solution.py
+++ b/solution.py
@@ -198,13 +198,14 @@
     def _(k):
         acc[k] = sum_of(0, k)
 
+    wait_bytes(pieces_in, state_recv)
     wait_bytes(incoming.at[1], part_recv.at[1])
 
     @pl.loop(0, n)
     def _(d):
         k = lax.rem(me + d + 1, n)
-        acc[k] = acc[k] + sum_of(1, k)
-        to_owner[k] = acc[k].astype(BF16)
+        total = acc[k] + sum_of(1, k)
+        to_owner[k] = total.astype(BF16)
 
         @pl.when(k != me)
         def _():
@@ -222,15 +223,11 @@
                 to_owner.at[k], slot_grad.at[me], owner_sem.at[1]
             ).start()
 
-    wait_bytes(pieces_in, state_recv)
-
-    @pl.loop(0, n)
-    def _(k):
         fresh[k] = adam(
             pieces_in[k, 0].astype(F32),
             pieces_in[k, 1].astype(F32),
             pieces_in[k, 2].astype(F32),
-            acc[k],
+            total,
         )[0].astype(BF16)
 
     for d in range(1, n + 1):

time: 27.2 us -> 27.2 us (level)
  no operation moved by 1% of the time
where the time goes in v8:
time: 27.2 us; the launch traced here: 27 us
  Pallas kernels  26.4 us (97%)
  between operations  0.64 us (2%)
    pallas_call x1, Pallas kernels, by_kernel(): pl.pallas_call(functools.partial(kernel, n), out_shape=tuple((pltpu.VMEM(...  25.5 us
    pallas_call x1, Pallas kernels, by_kernel(): pl.pallas_call(hand_over, out_shape=out_shape, in_specs=[any_spec] * 4, o...  0.91 us

profile of v8, /device:TPU:0, one launch (start us, length us, event | category | flops | bytes accessed | tf_op | source)
XLA Modules:
  0.0 27.0 jit_solution(15559953831834993987)
XLA Ops:
  0.6 25.5 %reduce_update_refresh.1 = (f32[1,32,1536]{2,1,0:T(8,128)S(1)}, f32[1,32,1536]{2,1,0:T(8,128)S(1)}, f32[1,32,1536]{2,1,0:T(8,128)S(1)}, bf16[2,32,1536]{2,1,0:T(8,128)(2,1)S(1)}) custom-call(bf16[1,2,128,1536]{3,2,1,0:T(8,128)(2,1)} %grads.1, f32[1,32,1536]{2,1,0:T(8,128)} %master.1, f32[1,32,1536]{2,1,0:T(8,128)} %moment.1, f32[1,32,1536]{2,1,0:T(8,128)} %second.1, ...), custom_call_target="tpu_custom_call" | custom-call | tf_op jit(solution)/shard_map/reduce_update_refresh/pallas_call | solution.py:290
  26.1 0.9 %hand_over.1 = (f32[1,32,1536]{2,1,0:T(8,128)}, f32[1,32,1536]{2,1,0:T(8,128)}, f32[1,32,1536]{2,1,0:T(8,128)}, bf16[2,32,1536]{2,1,0:T(8,128)(2,1)}) custom-call(f32[1,32,1536]{2,1,0:T(8,128)S(1)} %get-tuple-element.8.refs_0_, f32[1,32,1536]{2,1,0:T(8,128)S(1)} %get-tuple-element.9.refs_1_, f32[1,32,1536]{2,1,0:T(8,128)S(1)} %get-tuple-element.10.refs_2_, ...), custom_call_target="tpu_custom_call" | custom-call | tf_op jit(solution)/shard_map/hand_over/pallas_call | solution.py:325
